TPU v7x, 128 devices: a whole 4x4x4 slice. The times are simulated.
128 devices in a mesh: blk: 8 (over y, x_lo), grp: 16 (over z, x_hi, core).
Axes of the slice: x: 4 (x_hi: 2, x_lo: 2; x = x_hi * 2 + x_lo), y: 4, z: 4, core: 2. Of those that a mesh axis runs over, the one named last changes fastest.
Arguments:
- b_rows: bfloat16 [5120, 8, 896], P('grp', 'blk'), may hold values from -0.796875 to 0.796875
- aux_count: int32 [16], P('grp'), may hold values from 1 to 320, 5000 in all
- occ_pick: int32 [8], replicated, may hold values from 0 to 99, as said below
- eps_occ: float32 [100], replicated, may hold values from -2 to -0.5
- eps_vir: float32 [896], replicated, may hold values from 0.2 to 4
Outputs:
- gamma: bfloat16 [5120, 8, 896], P('grp', 'blk')
Inputs may be any that keep to these rules, and one draw needn't show every extreme that they name: `aux_count`: the counts sum to 5000. `occ_pick`: distinct entries; 0 and 99 both appear.
All inputs are finite; a program needn't handle non-finite values. No bound on the sum of `aux_count` on one device may be relied on, other than what follows from the above.
Results may differ from a plain program's by a relative error of at most 0.015.
Values may be sent and summed in bfloat16 or wider, within the bound.
A program may use at most 64 MiB of HBM per device.

v0:
```python
import jax
import jax.numpy as jnp
from jax import lax
from jax.sharding import PartitionSpec as P


def from_behind(value, axis, steps):
    count = lax.axis_size(axis)
    pairs = [(source, (source + steps) % count) for source in range(count)]
    return lax.ppermute(value, axis, pairs)


def on_device(b_rows, aux_count, occ_pick, eps_occ, eps_vir):
    aux_rows = b_rows.shape[0]
    nvirt = b_rows.shape[2]
    row_index = lax.broadcasted_iota(jnp.int32, (aux_rows, 1), 0)
    plain_rows = b_rows[:, 0, :]
    own_rows = jnp.where(row_index < aux_count[0], plain_rows, jnp.zeros_like(plain_rows))
    blocks = lax.axis_size("blk")
    position = lax.axis_index("blk")
    picked = jnp.take(eps_occ, occ_pick)
    own_energy = picked[position]

    def pair_amplitude(visitor, source):
        partial_value = lax.dot_general(
            own_rows, visitor, (((0,), (0,)), ((), ())), preferred_element_type=jnp.float32
        )
        pair_share = lax.psum_scatter(
            partial_value.astype(jnp.bfloat16), "grp", scatter_dimension=0, tiled=True
        )
        integral = lax.all_gather(pair_share, "grp", axis=0, tiled=True)
        full_pair = integral.astype(jnp.float32)
        energy_gap = own_energy + picked[source] - eps_vir[:, None] - eps_vir[None, :]
        return ((2.0 * full_pair - full_pair.T) / energy_gap).astype(jnp.bfloat16)

    def contribute(running, visitor, source):
        amplitude = pair_amplitude(visitor, source)
        return running + lax.dot_general(
            visitor, amplitude, (((1,), (1,)), ((), ())), preferred_element_type=jnp.float32
        )

    running = jnp.zeros((aux_rows, nvirt), jnp.float32)
    running = contribute(running, own_rows, position)

    def advance(stop_index, loop_state):
        running, visitor = loop_state
        visitor = from_behind(visitor, "blk", 1)
        running = contribute(running, visitor, (position - stop_index) % blocks)
        return (running, visitor)

    running, visitor = lax.fori_loop(1, blocks, advance, (running, own_rows))
    return running.astype(jnp.bfloat16)[:, None, :]


def solution(mesh):
    placed = (P("grp", "blk", None), P("grp"), P(), P(), P())
    return jax.shard_map(
        on_device, mesh=mesh, in_specs=placed, out_specs=P("grp", "blk", None), check_vma=False
    )
```

profile of v0, /device:TPU:1, one launch (start us, length us, event | category | flops | bytes accessed | tf_op | source)
XLA Modules:
  0.0 1150.3 jit_solution(5991315212146183849)
XLA Ops:
  7.3 3.6 convolution_convert_fusion.1
  11.0 72.6 %reduce-scatter.9.cloned.1.call-done = bf16[56,896]{1,0:T(8,128)(2,1)} async-done(((bf16[896,896]{1,0:T(8,128)(2,1)}), bf16[56,896]{1,0:T(8,128)(2,1)}) %reduce-scatter.9.cloned.1.call-update) | async-done | bytes 100368
  88.2 45.2 %all-gather.3.cloned.1.call-done = bf16[896,896]{1,0:T(8,128)(2,1)} async-done(((bf16[56,896]{1,0:T(8,128)(2,1)}), bf16[896,896]{1,0:T(8,128)(2,1)}) %all-gather.3.cloned.1.call-update) | async-done | bytes 1605648 | tf_op jit(solution)/shard_map/all_gather | solution.py:31
  133.4 2.8 copy.11
  136.2 3.9 fusion.14
  140.0 1001.6 %while.17 = (s32[]{:T(128)}, f32[320,896]{1,0:T(8,128)}, bf16[320,896]{1,0:T(8,128)(2,1)}, bf16[320,896]{1,0:T(8,128)(2,1)}, s32[]{:T(128)}, /*index=5*/f32[8]{0...) while((s32[]{:T(128)}, f32[320,896]{1,0:T(8,128)}, ...), condition=%wide.region_3.4_spmd, body=%wide.region_1.3_spmd.sunk | while | flops 1033511808 | bytes 31238584 | solution.py:51
  140.3 16.4 %collective-permute-done = bf16[320,896]{1,0:T(8,128)(2,1)S(1)} collective-permute-done((bf16[320,896]{1,0:T(8,128)(2,1)}, bf16[320,896]{1,0:T(8,128)(2,1)S(1)}, u32[]{:S(2)}, u32[]{:S(2)}) %collective-permute-start) | collective-permute-done | bytes 573472 | tf_op jit(solution)/shard_map/while/body/eval_jaxpr/ppermute | solution.py:10
  156.7 3.6 convolution_convert_fusion.3
  160.3 66.4 %reduce-scatter.11.cloned.1.call-done = bf16[56,896]{1,0:T(8,128)(2,1)} async-done(((bf16[896,896]{1,0:T(8,128)(2,1)}), bf16[56,896]{1,0:T(8,128)(2,1)}) %reduce-scatter.11.cloned.1.call-update) | async-done | bytes 100368 | tf_op jit(solution)/shard_map/while
  229.4 46.7 %all-gather.5.cloned.1.call-done = bf16[896,896]{1,0:T(8,128)(2,1)} async-done(((bf16[56,896]{1,0:T(8,128)(2,1)}), bf16[896,896]{1,0:T(8,128)(2,1)}) %all-gather.5.cloned.1.call-update) | async-done | bytes 1605648 | tf_op jit(solution)/shard_map/while/body/eval_jaxpr/all_gather | solution.py:31
  276.1 2.8 copy.13
  278.9 4.2 fusion.36
  283.4 16.4 %collective-permute-done = bf16[320,896]{1,0:T(8,128)(2,1)S(1)} collective-permute-done((bf16[320,896]{1,0:T(8,128)(2,1)}, bf16[320,896]{1,0:T(8,128)(2,1)S(1)}, u32[]{:S(2)}, u32[]{:S(2)}) %collective-permute-start) | collective-permute-done | bytes 573472 | tf_op jit(solution)/shard_map/while/body/eval_jaxpr/ppermute | solution.py:10
  299.8 3.6 convolution_convert_fusion.3
  303.4 66.3 %reduce-scatter.11.cloned.1.call-done = bf16[56,896]{1,0:T(8,128)(2,1)} async-done(((bf16[896,896]{1,0:T(8,128)(2,1)}), bf16[56,896]{1,0:T(8,128)(2,1)}) %reduce-scatter.11.cloned.1.call-update) | async-done | bytes 100368 | tf_op jit(solution)/shard_map/while
  372.4 46.7 %all-gather.5.cloned.1.call-done = bf16[896,896]{1,0:T(8,128)(2,1)} async-done(((bf16[56,896]{1,0:T(8,128)(2,1)}), bf16[896,896]{1,0:T(8,128)(2,1)}) %all-gather.5.cloned.1.call-update) | async-done | bytes 1605648 | tf_op jit(solution)/shard_map/while/body/eval_jaxpr/all_gather | solution.py:31
  419.1 2.8 copy.13
  421.9 4.2 fusion.36
  426.5 16.4 %collective-permute-done = bf16[320,896]{1,0:T(8,128)(2,1)S(1)} collective-permute-done((bf16[320,896]{1,0:T(8,128)(2,1)}, bf16[320,896]{1,0:T(8,128)(2,1)S(1)}, u32[]{:S(2)}, u32[]{:S(2)}) %collective-permute-start) | collective-permute-done | bytes 573472 | tf_op jit(solution)/shard_map/while/body/eval_jaxpr/ppermute | solution.py:10
  442.8 3.6 convolution_convert_fusion.3
  446.5 66.3 %reduce-scatter.11.cloned.1.call-done = bf16[56,896]{1,0:T(8,128)(2,1)} async-done(((bf16[896,896]{1,0:T(8,128)(2,1)}), bf16[56,896]{1,0:T(8,128)(2,1)}) %reduce-scatter.11.cloned.1.call-update) | async-done | bytes 100368 | tf_op jit(solution)/shard_map/while
  515.5 46.9 %all-gather.5.cloned.1.call-done = bf16[896,896]{1,0:T(8,128)(2,1)} async-done(((bf16[56,896]{1,0:T(8,128)(2,1)}), bf16[896,896]{1,0:T(8,128)(2,1)}) %all-gather.5.cloned.1.call-update) | async-done | bytes 1605648 | tf_op jit(solution)/shard_map/while/body/eval_jaxpr/all_gather | solution.py:31
  562.3 2.8 copy.13
  565.1 4.2 fusion.36
  569.6 16.4 %collective-permute-done = bf16[320,896]{1,0:T(8,128)(2,1)S(1)} collective-permute-done((bf16[320,896]{1,0:T(8,128)(2,1)}, bf16[320,896]{1,0:T(8,128)(2,1)S(1)}, u32[]{:S(2)}, u32[]{:S(2)}) %collective-permute-start) | collective-permute-done | bytes 573472 | tf_op jit(solution)/shard_map/while/body/eval_jaxpr/ppermute | solution.py:10
  586.0 3.6 convolution_convert_fusion.3
  589.6 66.4 %reduce-scatter.11.cloned.1.call-done = bf16[56,896]{1,0:T(8,128)(2,1)} async-done(((bf16[896,896]{1,0:T(8,128)(2,1)}), bf16[56,896]{1,0:T(8,128)(2,1)}) %reduce-scatter.11.cloned.1.call-update) | async-done | bytes 100368 | tf_op jit(solution)/shard_map/while
  658.7 46.7 %all-gather.5.cloned.1.call-done = bf16[896,896]{1,0:T(8,128)(2,1)} async-done(((bf16[56,896]{1,0:T(8,128)(2,1)}), bf16[896,896]{1,0:T(8,128)(2,1)}) %all-gather.5.cloned.1.call-update) | async-done | bytes 1605648 | tf_op jit(solution)/shard_map/while/body/eval_jaxpr/all_gather | solution.py:31
  705.4 2.8 copy.13
  708.2 4.2 fusion.36
  712.7 16.4 %collective-permute-done = bf16[320,896]{1,0:T(8,128)(2,1)S(1)} collective-permute-done((bf16[320,896]{1,0:T(8,128)(2,1)}, bf16[320,896]{1,0:T(8,128)(2,1)S(1)}, u32[]{:S(2)}, u32[]{:S(2)}) %collective-permute-start) | collective-permute-done | bytes 573472 | tf_op jit(solution)/shard_map/while/body/eval_jaxpr/ppermute | solution.py:10
  729.1 3.6 convolution_convert_fusion.3
  732.7 66.4 %reduce-scatter.11.cloned.1.call-done = bf16[56,896]{1,0:T(8,128)(2,1)} async-done(((bf16[896,896]{1,0:T(8,128)(2,1)}), bf16[56,896]{1,0:T(8,128)(2,1)}) %reduce-scatter.11.cloned.1.call-update) | async-done | bytes 100368 | tf_op jit(solution)/shard_map/while
  801.8 46.7 %all-gather.5.cloned.1.call-done = bf16[896,896]{1,0:T(8,128)(2,1)} async-done(((bf16[56,896]{1,0:T(8,128)(2,1)}), bf16[896,896]{1,0:T(8,128)(2,1)}) %all-gather.5.cloned.1.call-update) | async-done | bytes 1605648 | tf_op jit(solution)/shard_map/while/body/eval_jaxpr/all_gather | solution.py:31
  848.5 2.8 copy.13
  851.3 4.2 fusion.36
  855.8 16.4 %collective-permute-done = bf16[320,896]{1,0:T(8,128)(2,1)S(1)} collective-permute-done((bf16[320,896]{1,0:T(8,128)(2,1)}, bf16[320,896]{1,0:T(8,128)(2,1)S(1)}, u32[]{:S(2)}, u32[]{:S(2)}) %collective-permute-start) | collective-permute-done | bytes 573472 | tf_op jit(solution)/shard_map/while/body/eval_jaxpr/ppermute | solution.py:10
  872.2 3.6 convolution_convert_fusion.3
  875.8 66.4 %reduce-scatter.11.cloned.1.call-done = bf16[56,896]{1,0:T(8,128)(2,1)} async-done(((bf16[896,896]{1,0:T(8,128)(2,1)}), bf16[56,896]{1,0:T(8,128)(2,1)}) %reduce-scatter.11.cloned.1.call-update) | async-done | bytes 100368 | tf_op jit(solution)/shard_map/while
  944.9 46.7 %all-gather.5.cloned.1.call-done = bf16[896,896]{1,0:T(8,128)(2,1)} async-done(((bf16[56,896]{1,0:T(8,128)(2,1)}), bf16[896,896]{1,0:T(8,128)(2,1)}) %all-gather.5.cloned.1.call-update) | async-done | bytes 1605648 | tf_op jit(solution)/shard_map/while/body/eval_jaxpr/all_gather | solution.py:31
  991.6 2.8 copy.13
  994.4 4.2 fusion.36
  998.9 16.4 %collective-permute-done = bf16[320,896]{1,0:T(8,128)(2,1)S(1)} collective-permute-done((bf16[320,896]{1,0:T(8,128)(2,1)}, bf16[320,896]{1,0:T(8,128)(2,1)S(1)}, u32[]{:S(2)}, u32[]{:S(2)}) %collective-permute-start) | collective-permute-done | bytes 573472 | tf_op jit(solution)/shard_map/while/body/eval_jaxpr/ppermute | solution.py:10
  1015.3 3.6 convolution_convert_fusion.3
  1018.9 66.3 %reduce-scatter.11.cloned.1.call-done = bf16[56,896]{1,0:T(8,128)(2,1)} async-done(((bf16[896,896]{1,0:T(8,128)(2,1)}), bf16[56,896]{1,0:T(8,128)(2,1)}) %reduce-scatter.11.cloned.1.call-update) | async-done | bytes 100368 | tf_op jit(solution)/shard_map/while
  1087.9 46.7 %all-gather.5.cloned.1.call-done = bf16[896,896]{1,0:T(8,128)(2,1)} async-done(((bf16[56,896]{1,0:T(8,128)(2,1)}), bf16[896,896]{1,0:T(8,128)(2,1)}) %all-gather.5.cloned.1.call-update) | async-done | bytes 1605648 | tf_op jit(solution)/shard_map/while/body/eval_jaxpr/all_gather | solution.py:31
  1134.6 2.8 copy.13
  1137.4 4.2 fusion.36
  (94 shorter events, 17.6 us)
Async XLA Ops:
  6.5 77.1 %copy-start = (f32[100]{0:T(128)S(1)}, f32[100]{0:T(128)}, u32[]{:S(2)}) copy-start(f32[100]{0:T(128)} %param.10) | copy-start | bytes 1204
  6.5 79.8 %copy-start.3 = (bf16[320,1,896]{2,0,1:T(8,128)(2,1)S(1)}, bf16[320,1,896]{2,0,1:T(8,128)(2,1)}, u32[]{:S(2)}) copy-start(bf16[320,1,896]{2,0,1:T(8,128)(2,1)} %param.7) | copy-start | bytes 1720324
  6.5 77.1 %copy-start.5 = (s32[8]{0:T(128)S(1)}, s32[8]{0:T(128)}, u32[]{:S(2)}) copy-start(s32[8]{0:T(128)} %param.9) | copy-start | bytes 100
  6.5 77.1 %reduce-scatter.9.cloned.1.call-start = ((), (), s32[]{:S(2)}) async-start(), calls=%async_computation.3 | async-start | bytes 1705984
  7.3 80.9 %copy-start.4 = (f32[896]{0:T(1024)S(1)}, f32[896]{0:T(1024)}, u32[]{:S(2)}) copy-start(f32[896]{0:T(1024)} %param.11) | copy-start | bytes 10756
  11.0 122.4 %all-gather.3.cloned.1.call-start = ((), (), s32[]{:S(2)}) async-start(), calls=%async_computation.2 | async-start | bytes 1705984 | tf_op jit(solution)/shard_map/all_gather | solution.py:31
  86.5 0.8 copy-start.2
  140.0 86.7 %reduce-scatter.11.cloned.1.call-start = ((), (), s32[]{:S(2)}) async-start(), calls=%async_computation.4 | async-start | bytes 1705984 | tf_op jit(solution)/shard_map/while
  140.0 16.7 %collective-permute-start = (bf16[320,896]{1,0:T(8,128)(2,1)}, bf16[320,896]{1,0:T(8,128)(2,1)S(1)}, u32[]{:S(2)}, u32[]{:S(2)}) collective-permute-start(bf16[320,896]{1,0:T(8,128)(2,1)} %get-tuple-element.284), channel_id=1, source_target_pairs={{0,16},{16,32},{32,48},{48,64},{64,80},{80,96},{96,112},{112,0},{1... | collective-permute-start | bytes 1720328 | tf_op jit(solution)/shard_map/while/body/eval_jaxpr/ppermute | solution.py:10
  156.7 72.7 %copy-start.1 = (bf16[320,896]{1,0:T(8,128)(2,1)}, bf16[320,896]{1,0:T(8,128)(2,1)S(1)}, u32[]{:S(2)}) copy-start(bf16[320,896]{1,0:T(8,128)(2,1)S(1)} %collective-permute-done) | copy-start | bytes 1720324 | tf_op jit(solution)/shard_map/while
  160.3 115.8 %all-gather.5.cloned.1.call-start = ((), (), s32[]{:S(2)}) async-start(), calls=%async_computation.5 | async-start | bytes 1705984 | tf_op jit(solution)/shard_map/while/body/eval_jaxpr/all_gather | solution.py:31
  283.2 86.6 %reduce-scatter.11.cloned.1.call-start = ((), (), s32[]{:S(2)}) async-start(), calls=%async_computation.4 | async-start | bytes 1705984 | tf_op jit(solution)/shard_map/while
  283.2 16.7 %collective-permute-start = (bf16[320,896]{1,0:T(8,128)(2,1)}, bf16[320,896]{1,0:T(8,128)(2,1)S(1)}, u32[]{:S(2)}, u32[]{:S(2)}) collective-permute-start(bf16[320,896]{1,0:T(8,128)(2,1)} %get-tuple-element.284), channel_id=1, source_target_pairs={{0,16},{16,32},{32,48},{48,64},{64,80},{80,96},{96,112},{112,0},{1... | collective-permute-start | bytes 1720328 | tf_op jit(solution)/shard_map/while/body/eval_jaxpr/ppermute | solution.py:10
  299.8 72.6 %copy-start.1 = (bf16[320,896]{1,0:T(8,128)(2,1)}, bf16[320,896]{1,0:T(8,128)(2,1)S(1)}, u32[]{:S(2)}) copy-start(bf16[320,896]{1,0:T(8,128)(2,1)S(1)} %collective-permute-done) | copy-start | bytes 1720324 | tf_op jit(solution)/shard_map/while
  303.4 115.8 %all-gather.5.cloned.1.call-start = ((), (), s32[]{:S(2)}) async-start(), calls=%async_computation.5 | async-start | bytes 1705984 | tf_op jit(solution)/shard_map/while/body/eval_jaxpr/all_gather | solution.py:31
  426.2 86.6 %reduce-scatter.11.cloned.1.call-start = ((), (), s32[]{:S(2)}) async-start(), calls=%async_computation.4 | async-start | bytes 1705984 | tf_op jit(solution)/shard_map/while
  426.2 16.7 %collective-permute-start = (bf16[320,896]{1,0:T(8,128)(2,1)}, bf16[320,896]{1,0:T(8,128)(2,1)S(1)}, u32[]{:S(2)}, u32[]{:S(2)}) collective-permute-start(bf16[320,896]{1,0:T(8,128)(2,1)} %get-tuple-element.284), channel_id=1, source_target_pairs={{0,16},{16,32},{32,48},{48,64},{64,80},{80,96},{96,112},{112,0},{1... | collective-permute-start | bytes 1720328 | tf_op jit(solution)/shard_map/while/body/eval_jaxpr/ppermute | solution.py:10
  442.8 72.6 %copy-start.1 = (bf16[320,896]{1,0:T(8,128)(2,1)}, bf16[320,896]{1,0:T(8,128)(2,1)S(1)}, u32[]{:S(2)}) copy-start(bf16[320,896]{1,0:T(8,128)(2,1)S(1)} %collective-permute-done) | copy-start | bytes 1720324 | tf_op jit(solution)/shard_map/while
  446.4 115.9 %all-gather.5.cloned.1.call-start = ((), (), s32[]{:S(2)}) async-start(), calls=%async_computation.5 | async-start | bytes 1705984 | tf_op jit(solution)/shard_map/while/body/eval_jaxpr/all_gather | solution.py:31
  569.3 86.7 %reduce-scatter.11.cloned.1.call-start = ((), (), s32[]{:S(2)}) async-start(), calls=%async_computation.4 | async-start | bytes 1705984 | tf_op jit(solution)/shard_map/while
  569.3 16.7 %collective-permute-start = (bf16[320,896]{1,0:T(8,128)(2,1)}, bf16[320,896]{1,0:T(8,128)(2,1)S(1)}, u32[]{:S(2)}, u32[]{:S(2)}) collective-permute-start(bf16[320,896]{1,0:T(8,128)(2,1)} %get-tuple-element.284), channel_id=1, source_target_pairs={{0,16},{16,32},{32,48},{48,64},{64,80},{80,96},{96,112},{112,0},{1... | collective-permute-start | bytes 1720328 | tf_op jit(solution)/shard_map/while/body/eval_jaxpr/ppermute | solution.py:10
  586.0 72.7 %copy-start.1 = (bf16[320,896]{1,0:T(8,128)(2,1)}, bf16[320,896]{1,0:T(8,128)(2,1)S(1)}, u32[]{:S(2)}) copy-start(bf16[320,896]{1,0:T(8,128)(2,1)S(1)} %collective-permute-done) | copy-start | bytes 1720324 | tf_op jit(solution)/shard_map/while
  589.6 115.8 %all-gather.5.cloned.1.call-start = ((), (), s32[]{:S(2)}) async-start(), calls=%async_computation.5 | async-start | bytes 1705984 | tf_op jit(solution)/shard_map/while/body/eval_jaxpr/all_gather | solution.py:31
  712.4 86.7 %reduce-scatter.11.cloned.1.call-start = ((), (), s32[]{:S(2)}) async-start(), calls=%async_computation.4 | async-start | bytes 1705984 | tf_op jit(solution)/shard_map/while
  712.4 16.7 %collective-permute-start = (bf16[320,896]{1,0:T(8,128)(2,1)}, bf16[320,896]{1,0:T(8,128)(2,1)S(1)}, u32[]{:S(2)}, u32[]{:S(2)}) collective-permute-start(bf16[320,896]{1,0:T(8,128)(2,1)} %get-tuple-element.284), channel_id=1, source_target_pairs={{0,16},{16,32},{32,48},{48,64},{64,80},{80,96},{96,112},{112,0},{1... | collective-permute-start | bytes 1720328 | tf_op jit(solution)/shard_map/while/body/eval_jaxpr/ppermute | solution.py:10
  729.1 72.7 %copy-start.1 = (bf16[320,896]{1,0:T(8,128)(2,1)}, bf16[320,896]{1,0:T(8,128)(2,1)S(1)}, u32[]{:S(2)}) copy-start(bf16[320,896]{1,0:T(8,128)(2,1)S(1)} %collective-permute-done) | copy-start | bytes 1720324 | tf_op jit(solution)/shard_map/while
  732.7 115.8 %all-gather.5.cloned.1.call-start = ((), (), s32[]{:S(2)}) async-start(), calls=%async_computation.5 | async-start | bytes 1705984 | tf_op jit(solution)/shard_map/while/body/eval_jaxpr/all_gather | solution.py:31
  855.5 86.7 %reduce-scatter.11.cloned.1.call-start = ((), (), s32[]{:S(2)}) async-start(), calls=%async_computation.4 | async-start | bytes 1705984 | tf_op jit(solution)/shard_map/while
  855.5 16.7 %collective-permute-start = (bf16[320,896]{1,0:T(8,128)(2,1)}, bf16[320,896]{1,0:T(8,128)(2,1)S(1)}, u32[]{:S(2)}, u32[]{:S(2)}) collective-permute-start(bf16[320,896]{1,0:T(8,128)(2,1)} %get-tuple-element.284), channel_id=1, source_target_pairs={{0,16},{16,32},{32,48},{48,64},{64,80},{80,96},{96,112},{112,0},{1... | collective-permute-start | bytes 1720328 | tf_op jit(solution)/shard_map/while/body/eval_jaxpr/ppermute | solution.py:10
  872.2 72.7 %copy-start.1 = (bf16[320,896]{1,0:T(8,128)(2,1)}, bf16[320,896]{1,0:T(8,128)(2,1)S(1)}, u32[]{:S(2)}) copy-start(bf16[320,896]{1,0:T(8,128)(2,1)S(1)} %collective-permute-done) | copy-start | bytes 1720324 | tf_op jit(solution)/shard_map/while
  875.8 115.8 %all-gather.5.cloned.1.call-start = ((), (), s32[]{:S(2)}) async-start(), calls=%async_computation.5 | async-start | bytes 1705984 | tf_op jit(solution)/shard_map/while/body/eval_jaxpr/all_gather | solution.py:31
  998.6 86.6 %reduce-scatter.11.cloned.1.call-start = ((), (), s32[]{:S(2)}) async-start(), calls=%async_computation.4 | async-start | bytes 1705984 | tf_op jit(solution)/shard_map/while
  998.7 16.7 %collective-permute-start = (bf16[320,896]{1,0:T(8,128)(2,1)}, bf16[320,896]{1,0:T(8,128)(2,1)S(1)}, u32[]{:S(2)}, u32[]{:S(2)}) collective-permute-start(bf16[320,896]{1,0:T(8,128)(2,1)} %get-tuple-element.284), channel_id=1, source_target_pairs={{0,16},{16,32},{32,48},{48,64},{64,80},{80,96},{96,112},{112,0},{1... | collective-permute-start | bytes 1720328 | tf_op jit(solution)/shard_map/while/body/eval_jaxpr/ppermute | solution.py:10
  1015.3 72.6 %copy-start.1 = (bf16[320,896]{1,0:T(8,128)(2,1)}, bf16[320,896]{1,0:T(8,128)(2,1)S(1)}, u32[]{:S(2)}) copy-start(bf16[320,896]{1,0:T(8,128)(2,1)S(1)} %collective-permute-done) | copy-start | bytes 1720324 | tf_op jit(solution)/shard_map/while
  1018.9 115.7 %all-gather.5.cloned.1.call-start = ((), (), s32[]{:S(2)}) async-start(), calls=%async_computation.5 | async-start | bytes 1705984 | tf_op jit(solution)/shard_map/while/body/eval_jaxpr/all_gather | solution.py:31
Sparse Core Ops, SparseCore 0:
  11.4 72.2 reduce-scatter.8
  86.3 47.0 all-gather.2
  160.4 66.3 reduce-scatter.10
  229.0 47.0 all-gather.4
  303.5 66.2 reduce-scatter.10
  372.0 47.0 all-gather.4
  446.5 66.2 reduce-scatter.10
  515.2 47.0 all-gather.4
  589.7 66.2 reduce-scatter.10
  658.3 47.0 all-gather.4
  732.8 66.2 reduce-scatter.10
  801.4 47.0 all-gather.4
  875.9 66.2 reduce-scatter.10
  944.5 47.0 all-gather.4
  1019.0 66.2 reduce-scatter.10
  1087.5 47.0 all-gather.4
where the time goes:
time: 1150 us
  waiting for transfers between devices  1020 us (89%)
  matrix products  62 us (5%)
  local copies, waits for them, and re-layouts  34.9 us (3%)
  between operations  15.3 us (1%)
    while x21, waiting for transfers between devices  465 us
    all_gather x8, waiting for transfers between devices, pair_amplitude(): integral = lax.all_gather(pair_share, 'grp', axis=0, tiled=True)  372 us
    ppermute x7, waiting for transfers between devices, from_behind(): return lax.ppermute(value, axis, pairs)  115 us
    unnamed x3, waiting for transfers between devices  72.6 us
    dot_general x8, matrix products, contribute(): lax.dot_general(visitor, amplitude, (((1,), (1,)), ((), ())), preferred_e...  33.5 us
    dot_general x8, matrix products, pair_amplitude(): lax.dot_general(own_rows, visitor, (((0,), (0,)), ((), ())), preferred_el...  28.5 us
  transfers between devices with their start and end apart: 23, of which 23 were waited for; matrix products, arithmetic and copies ran while one was open for 1% of the time, Pallas kernels for 0%

commit v1 on v0

v1 whole, which is shorter than its diff:
```python
import functools

import jax
import jax.numpy as jnp
from jax import lax
from jax.experimental import pallas as pl
from jax.experimental.pallas import tpu as pltpu
from jax.sharding import PartitionSpec as P

MESH = pl.DeviceIdType.MESH
ROWS, NVIR = 320, 896
HALF = NVIR // 2
PIECE = HALF // 4
CUT = 64
WINDOW = 512
JOBS = 5
OWN, NEXT, AFTER, PARTNER = range(4)


def device_at(x, y, z, core):
    return (y * 2 + x % 2, z * 4 + (x // 2) * 2 + core)


def kernel(
    count, pick, occ, vir, b_ref, out,
    rows, flipped, acc, amp, virc, partial, whole, half_whole,
    z1_up, z1_down, z2_up, z2_down, mine, other, back_out, back_in,
    send, recv, b_send, b_recv,
):
    blk, grp = lax.axis_index("blk"), lax.axis_index("grp")
    y, lo = blk // 2, blk % 2
    z, core = grp // 4, grp % 2
    x = ((grp // 2) % 2) * 2 + lo

    sibling = device_at(x, y, z, 1 - core)
    below, above = device_at(x, (y + 3) % 4, z, core), device_at(x, (y + 1) % 4, z, core)
    across = device_at(x, (y + 2) % 4, z, core)
    partner = device_at(x + 1 - 2 * lo, y, z, core)
    far = device_at((x + 2) % 4, y, z, core)
    up, down = device_at(x, y, (z + 1) % 4, core), device_at(x, y, (z + 3) % 4, core)

    own_part = pl.ds(pl.multiple_of(core * ROWS, 16), ROWS)
    started = []

    def start(src, dst, sends, receives, device):
        copy = pltpu.make_async_remote_copy(
            src_ref=src, dst_ref=dst, send_sem=sends, recv_sem=receives,
            device_id=device, device_id_type=MESH,
        )
        copy.start()
        started.append(copy)
        return copy

    line = lax.broadcasted_iota(jnp.int32, (ROWS, NVIR), 0)
    live = jnp.where(line < count[0], b_ref[...].astype(jnp.float32), 0.0).astype(jnp.bfloat16)
    rows[OWN, own_part, :] = live
    half_whole[...] = jnp.zeros_like(half_whole)
    acc[...] = jnp.zeros_like(acc)

    barrier = pltpu.get_barrier_semaphore()
    everyone = (sibling, below, above, across, partner, far, up, down)
    for device in everyone:
        pl.semaphore_signal(barrier, inc=1, device_id=device, device_id_type=MESH)
    pl.semaphore_wait(barrier, len(everyone))

    def spread(slot, index, device):
        return start(
            rows.at[OWN, own_part], rows.at[slot, own_part], b_send.at[index], b_recv.at[index], device
        )

    def pass_on(slot, index):
        return start(
            rows.at[slot, own_part], rows.at[slot, own_part], b_send.at[index], b_recv.at[index], sibling
        )

    own_shared = spread(OWN, 0, sibling)
    next_moved = spread(NEXT, 1, below)
    partner_moved = spread(PARTNER, 2, partner)

    virc[...] = jnp.transpose(jnp.broadcast_to(vir[...], (128, NVIR)))

    def energy(position):
        return occ[pick[position]]

    e_own = energy(blk)
    e_next = energy(((y + 1) % 4) * 2 + lo)
    e_after = energy(((y + 2) % 4) * 2 + lo)
    e_partner = energy(y * 2 + 1 - lo)
    low = lo == 0
    pair_energy = (
        e_own + e_own,
        e_own + e_next,
        e_partner + jnp.where(low, e_own, e_next),
        e_partner + jnp.where(low, e_next, e_after),
        e_own + e_after,
    )
    left = (OWN, OWN, PARTNER, PARTNER, OWN)
    right = (OWN, NEXT, lo, 1 + lo, AFTER)
    turned = y // 2

    def half_rows(which):
        return which * HALF

    def span(which, piece, first=0, size=PIECE):
        return pl.ds(pl.multiple_of(which * HALF + piece * PIECE + first, 16), size)

    def part(piece, first=0, size=PIECE):
        return pl.ds(pl.multiple_of(piece * PIECE + first, 16), size)

    z_up, z_down, z_far = (z + 1) % 4, (z + 3) % 4, (z + 2) % 4

    def window(which):
        flip = (which + turned) % 2
        return pl.ds(pl.multiple_of(flip * (NVIR - WINDOW), 128), WINDOW)

    def width(job):
        return WINDOW if job == 4 else NVIR

    def cols(job):
        return pl.ds(0, width(job))

    def full(job, lines):
        if job == 4:
            return half_whole.at[lines, window(core)]
        return whole.at[job, lines]

    def turn(slot, index):
        def body(step, carry):
            at = pl.ds(pl.multiple_of(step * 128, 128), 128)
            flipped[index, :, at] = jnp.transpose(rows[slot, at, :].astype(jnp.float32)).astype(jnp.bfloat16)
            return carry

        lax.fori_loop(0, 2 * ROWS // 128, body, 0)

    flip_index = (0, 0, 1, 1, 0)
    copies = {}

    def stage0(job):
        lhs = flipped[flip_index[job], pl.ds(pl.multiple_of(core * HALF, 16), HALF), :]
        rhs = rows[right[job], :, window(core)] if job == 4 else rows[right[job]]
        partial[job, :, cols(job)] = jnp.dot(lhs, rhs, preferred_element_type=jnp.float32).astype(jnp.bfloat16)
        copies[job, 0] = start(
            partial.at[job, part(z_far, 0, CUT), cols(job)], z1_up.at[job, :, cols(job)],
            send.at[job, 0], recv.at[job, 0], up,
        )
        copies[job, 1] = start(
            partial.at[job, part(z_far, CUT, PIECE - CUT), cols(job)], z1_down.at[job, :, cols(job)],
            send.at[job, 1], recv.at[job, 1], down,
        )

    def add(job, where, arrived):
        partial[job, where, cols(job)] = (
            partial[job, where, cols(job)].astype(jnp.float32) + arrived[job, :, cols(job)].astype(jnp.float32)
        ).astype(jnp.bfloat16)

    def stage1(job):
        copies[job, 0].wait_recv()
        add(job, part(z_up, 0, CUT), z1_up)
        copies[job, 2] = start(
            partial.at[job, part(z_up), cols(job)], z2_up.at[job, :, cols(job)],
            send.at[job, 2], recv.at[job, 2], up,
        )
        copies[job, 1].wait_recv()
        add(job, part(z_down, CUT, PIECE - CUT), z1_down)
        copies[job, 3] = start(
            partial.at[job, part(z_down), cols(job)], z2_down.at[job, :, cols(job)],
            send.at[job, 3], recv.at[job, 3], down,
        )

    def stage2(job):
        copies[job, 2].wait_recv()
        copies[job, 3].wait_recv()
        w = cols(job)
        mine[job, :, w] = (
            partial[job, part(z), w].astype(jnp.float32)
            + z2_up[job, :, w].astype(jnp.float32)
            + z2_down[job, :, w].astype(jnp.float32)
        ).astype(jnp.bfloat16)
        copies[job, 4] = start(
            mine.at[job, :, w], other.at[job, :, w], send.at[job, 4], recv.at[job, 4], far
        )

    def same(job, lines, index, device):
        copies[job, index] = start(
            full(job, lines), full(job, lines), send.at[job, index], recv.at[job, index], device
        )

    def stage3(job):
        copies[job, 4].wait_recv()
        w = cols(job)
        total = (mine[job, :, w].astype(jnp.float32) + other[job, :, w].astype(jnp.float32)).astype(jnp.bfloat16)
        if job == 4:
            half_whole[span(core, z), window(core)] = total
        else:
            whole[job, span(core, z), :] = total
        same(job, span(core, z), 5, up)
        same(job, span(core, z), 6, down)
        same(job, span(core, z), 7, sibling)

    def stage4(job):
        copies[job, 5].wait_recv()
        same(job, span(core, z_down, 0, CUT), 8, up)
        same(job, span(core, z_down), 9, sibling)
        copies[job, 6].wait_recv()
        same(job, span(core, z_up, CUT, PIECE - CUT), 10, down)
        same(job, span(core, z_up), 11, sibling)

    def stage5(job):
        copies[job, 8].wait_recv()
        copies[job, 10].wait_recv()
        same(job, span(core, z_far), 12, sibling)

    def stage6(job):
        for index in (7, 9, 11, 12):
            copies[job, index].wait_recv()
        source = half_whole if job == 4 else whole.at[job]
        base = pair_energy[job]

        def body(step, carry):
            at = pl.ds(pl.multiple_of(step * 128, 128), 128)
            plain = source[at, :].astype(jnp.float32)
            swapped = jnp.transpose(source[:, at].astype(jnp.float32))
            gap = (base - virc[at, 0:1]) - vir[...]
            value = (2.0 * plain - swapped) / gap
            if job == 4:
                a = lax.broadcasted_iota(jnp.int32, (128, NVIR), 0) + step * 128
                b = lax.broadcasted_iota(jnp.int32, (128, NVIR), 1)
                crossed = (a >= HALF).astype(jnp.int32) + (b >= HALF).astype(jnp.int32)
                value = jnp.where((crossed + turned) % 2 == 0, value, 0.0)
            amp[at, :] = value.astype(jnp.bfloat16)
            return carry

        lax.fori_loop(0, NVIR // 128, body, 0)
        acc[left[job]] = acc[left[job]] + lax.dot_general(
            rows[right[job], own_part, :], amp[...], (((1,), (1,)), ((), ())), preferred_element_type=jnp.float32
        )
        if job > 0:
            acc[right[job]] = acc[right[job]] + jnp.dot(
                rows[left[job], own_part, :], amp[...], preferred_element_type=jnp.float32
            )

    def give_back(slot, index, device):
        back_out[index] = acc[slot].astype(jnp.bfloat16)
        return start(back_out.at[index], back_in.at[index], b_send.at[index + 7], b_recv.at[index + 7], device)

    own_shared.wait_recv()
    turn(OWN, 0)
    stage0(0)
    stage1(0)
    next_moved.wait_recv()
    next_shared = pass_on(NEXT, 3)
    after_moved = spread(AFTER, 4, across)
    stage2(0)
    next_shared.wait_recv()
    stage0(1)
    partner_moved.wait_recv()
    partner_shared = pass_on(PARTNER, 5)
    stage3(0)
    stage1(1)
    partner_shared.wait_recv()
    turn(PARTNER, 1)
    stage0(2)
    stage4(0)
    stage2(1)
    stage1(2)
    after_moved.wait_recv()
    after_shared = pass_on(AFTER, 6)
    stage5(0)
    stage3(1)
    after_shared.wait_recv()
    stage0(3)
    stage2(2)
    stage1(3)
    stage0(4)
    stage6(0)
    stage4(1)
    stage3(2)
    stage2(3)
    stage1(4)
    stage5(1)
    stage4(2)
    stage3(3)
    stage2(4)
    stage6(1)
    stage5(2)
    stage4(3)
    stage3(4)
    stage6(2)
    stage5(3)
    stage4(4)
    stage6(3)
    next_back = give_back(NEXT, 0, above)
    partner_back = give_back(PARTNER, 1, partner)
    stage5(4)
    stage6(4)
    after_back = give_back(AFTER, 2, across)
    next_back.wait_recv()
    partner_back.wait_recv()
    total = acc[OWN] + back_in[0].astype(jnp.float32) + back_in[1].astype(jnp.float32)
    after_back.wait_recv()
    out[...] = (total + back_in[2].astype(jnp.float32)).astype(jnp.bfloat16)
    for copy in started:
        copy.wait_send()


def on_device(b_rows, aux_count, occ_pick, eps_occ, eps_vir):
    bf16, f32 = jnp.bfloat16, jnp.float32
    smem, vmem = pl.BlockSpec(memory_space=pltpu.SMEM), pl.BlockSpec(memory_space=pltpu.VMEM)
    dma = pltpu.SemaphoreType.DMA
    gamma = pl.pallas_call(
        kernel,
        out_shape=jax.ShapeDtypeStruct((ROWS, NVIR), bf16),
        in_specs=[smem, smem, smem, vmem, vmem],
        out_specs=vmem,
        scratch_shapes=[
            pltpu.VMEM((4, 2 * ROWS, NVIR), bf16),
            pltpu.VMEM((2, NVIR, 2 * ROWS), bf16),
            pltpu.VMEM((4, ROWS, NVIR), f32),
            pltpu.VMEM((NVIR, NVIR), bf16),
            pltpu.VMEM((NVIR, 128), f32),
            pltpu.VMEM((JOBS, HALF, NVIR), bf16),
            pltpu.VMEM((JOBS - 1, NVIR, NVIR), bf16),
            pltpu.VMEM((NVIR, NVIR), bf16),
            pltpu.VMEM((JOBS, CUT, NVIR), bf16),
            pltpu.VMEM((JOBS, PIECE - CUT, NVIR), bf16),
            pltpu.VMEM((JOBS, PIECE, NVIR), bf16),
            pltpu.VMEM((JOBS, PIECE, NVIR), bf16),
            pltpu.VMEM((JOBS, PIECE, NVIR), bf16),
            pltpu.VMEM((JOBS, PIECE, NVIR), bf16),
            pltpu.VMEM((3, ROWS, NVIR), bf16),
            pltpu.VMEM((3, ROWS, NVIR), bf16),
            dma((JOBS, 13)), dma((JOBS, 13)), dma((10,)), dma((10,)),
        ],
        compiler_params=pltpu.CompilerParams(
            collective_id=0, has_side_effects=True, vmem_limit_bytes=56 * 2**20
        ),
    )(aux_count, occ_pick, eps_occ, eps_vir.reshape(1, NVIR), b_rows[:, 0, :])
    return gamma[:, None, :]


def solution(mesh):
    placed = (P("grp", "blk", None), P("grp"), P(), P(), P())
    return jax.shard_map(
        on_device, mesh=mesh, in_specs=placed, out_specs=P("grp", "blk", None), check_vma=False
    )
```

time: 1150 us -> 123 us (0.11)
  waiting for transfers between devices: 1020 us -> 0 us
  Pallas kernels: 0 us -> 119 us
  matrix products: 62 us -> 0 us
  local copies, waits for them, and re-layouts: 34.9 us -> 3.18 us
  between operations: 15.3 us -> 0.66 us
    while x21 -> x0, waiting for transfers between devices: 465 us -> none
    all_gather x8 -> x0, waiting for transfers between devices: 372 us -> none  [pair_amplitude(): integral = lax.all_gather(pair_share, 'grp', axis=0, tiled=True)]
    pallas_call x0 -> x1, Pallas kernels: none -> 119 us  [on_device(): pl.pallas_call(kernel, out_shape=jax.ShapeDtypeStruct((ROWS, NVIR), bf16)...]
    ppermute x7 -> x0, waiting for transfers between devices: 115 us -> none  [from_behind(): return lax.ppermute(value, axis, pairs)]
    unnamed x3 -> x0, waiting for transfers between devices: 72.6 us -> none
    dot_general x16 -> x0, matrix products: 62 us -> none  [the longest x8 33.5 us: contribute(): lax.dot_general(visitor, amplitude, (((1,), (1,)), ((), ())), preferred_e...]
    convert_element_type x8 -> x0, local copies, waits for them, and re-layouts: 22.3 us -> none  [pair_amplitude(): full_pair = integral.astype(jnp.float32)]
  transfers between devices with their start and end apart: 23 -> 0, of which waited for: 23 -> 0; matrix products, arithmetic and copies ran while one was open for 1% -> 0% of each run, Pallas kernels for 0% -> 0%
where the time goes in v1:
time: 123 us
  Pallas kernels  119 us (97%)
  local copies, waits for them, and re-layouts  3.18 us (3%)
    pallas_call x1, Pallas kernels, on_device(): pl.pallas_call(kernel, out_shape=jax.ShapeDtypeStruct((ROWS, NVIR), bf16)...  119 us

profile of v1, /device:TPU:1, one launch (start us, length us, event | category | flops | bytes accessed | tf_op | source)
XLA Modules:
  0.0 123.1 jit_solution(16186538956818307101)
XLA Ops:
  0.7 1.3 %reshape.3.vir = f32[1,896]{1,0:T(1,128)} reshape(f32[896]{0:T(1024)} %param.9) | data formatting | bytes 7168 | tf_op jit(solution)/shard_map/reshape | solution.py:337
  1.9 119.2 %shard_map.55 = bf16[320,896]{1,0:T(8,128)(2,1)} custom-call(s32[1]{0:T(128)S(6)} %copy.7.count, s32[8]{0:T(128)} %pick.1, f32[100]{0:T(128)} %occ.1, f32[1,896]{1,0:T(1,128)} %reshape.3.vir, bf16[320,896]{1,0:T(8,128)(2,1)} %bitcast.3), custom_call_target="tpu_custom_call" | custom-call | tf_op jit(solution)/shard_map/pallas_call | solution.py:310
  121.2 1.9 %copy.8 = bf16[320,1,896]{2,0,1:T(8,128)(2,1)} copy(bf16[320,1,896]{2,0,1:T(8,128)(2,1)} %bitcast.2) | data formatting | bytes 1146880

commit v2 on v1

v2 whole, which is shorter than its diff:
```python
import jax
import jax.numpy as jnp
from jax import lax
from jax.experimental import pallas as pl
from jax.experimental.pallas import tpu as pltpu
from jax.sharding import PartitionSpec as P

MESH = pl.DeviceIdType.MESH
ROWS, NVIR = 320, 896
HALF = NVIR // 2
PIECE = HALF // 4
CUT = 64
SPLIT = 512
WINDOW = 512
OWN, NEXT, PREV, MATE = range(4)
JOBS = 5
CHUNKS = ((0, 0, 896), (1, 0, 896), (2, 0, 896), (3, 0, 896), (4, 0, 512))


def device_at(x, y, z, core):
    return (y * 2 + x % 2, z * 4 + (x // 2) * 2 + core)


def kernel(
    count, pick, occ, vir, b_ref, out,
    rows, flipped, acc, amp, virc, partial, whole, half_whole,
    z1_up, z1_down, z2_up, z2_down, mine, other, back_out, back_in,
    send, recv, b_send, b_recv,
):
    blk, grp = lax.axis_index("blk"), lax.axis_index("grp")
    y, lo = blk // 2, blk % 2
    z, core = grp // 4, grp % 2
    x = ((grp // 2) % 2) * 2 + lo
    y_up, y_down = (y + 1) % 4, (y + 3) % 4

    sibling = device_at(x, y, z, 1 - core)
    above, below = device_at(x, y_up, z, core), device_at(x, y_down, z, core)
    partner = device_at(x + 1 - 2 * lo, y, z, core)
    diagonal = device_at(x + 1 - 2 * lo, (y + 3 + 2 * lo) % 4, z, core)
    giver = device_at(x + 1 - 2 * lo, (y + lo) % 4, z, core)
    far = device_at((x + 2) % 4, y, z, core)
    up, down = device_at(x, y, (z + 1) % 4, core), device_at(x, y, (z + 3) % 4, core)

    own_part = pl.ds(pl.multiple_of(core * ROWS, 16), ROWS)
    started = []

    def remote(src, dst, sends, receives, device):
        copy = pltpu.make_async_remote_copy(
            src_ref=src, dst_ref=dst, send_sem=sends, recv_sem=receives,
            device_id=device, device_id_type=MESH,
        )
        started.append(copy)
        return copy

    def start(*where):
        copy = remote(*where)
        copy.start()
        return copy

    line = lax.broadcasted_iota(jnp.int32, (ROWS, NVIR), 0)
    live = jnp.where(line < count[0], b_ref[...].astype(jnp.float32), 0.0).astype(jnp.bfloat16)
    rows[OWN, own_part, :] = live
    half_whole[...] = jnp.zeros_like(half_whole)

    barrier = pltpu.get_barrier_semaphore()
    everyone = (sibling, above, below, partner, diagonal, far, up, down)
    for device in everyone:
        pl.semaphore_signal(barrier, inc=1, device_id=device, device_id_type=MESH)
    pl.semaphore_wait(barrier, len(everyone))

    first, second = pl.ds(0, SPLIT), pl.ds(SPLIT, NVIR - SPLIT)
    everything = pl.ds(0, NVIR)

    def spread(slot, columns, index, device):
        return start(
            rows.at[OWN, own_part, columns], rows.at[slot, own_part, columns],
            b_send.at[index], b_recv.at[index], device,
        )

    def pass_on(slot, columns, index):
        return start(
            rows.at[slot, own_part, columns], rows.at[slot, own_part, columns],
            b_send.at[index], b_recv.at[index], sibling,
        )

    def to_partner(columns, index):
        return remote(
            rows.at[(1 - lo) * NEXT, own_part, columns], rows.at[MATE, own_part, columns],
            b_send.at[index], b_recv.at[index], partner,
        )

    copies = {}
    copies["own"] = spread(OWN, everything, 0, sibling)
    copies["next a"] = spread(NEXT, first, 1, below)
    copies["next b"] = spread(NEXT, second, 2, below)
    copies["prev"] = spread(PREV, everything, 3, above)
    copies["mate a"] = to_partner(first, 4)
    copies["mate b"] = to_partner(second, 5)

    @pl.when(lo == 1)
    def _():
        copies["mate a"].start()
        copies["mate b"].start()

    acc[...] = jnp.zeros_like(acc)
    virc[...] = jnp.transpose(jnp.broadcast_to(vir[...], (128, NVIR)))

    def energy(position):
        return occ[pick[position]]

    e_own = energy(blk)
    e_next = energy(y_up * 2 + lo)
    e_prev = energy(y_down * 2 + lo)
    e_mate = energy(((y + lo) % 4) * 2 + 1 - lo)
    pair_energy = (e_own + e_own, e_own + e_next, e_mate + e_own, e_mate + e_prev, e_prev + e_next)
    left = (OWN, OWN, MATE, MATE, PREV)
    right = (OWN, NEXT, OWN, PREV, NEXT)
    turned = y // 2

    def span(which, piece, first=0, size=PIECE):
        return pl.ds(pl.multiple_of(which * HALF + piece * PIECE + first, 16), size)

    def part(piece, first=0, size=PIECE):
        return pl.ds(pl.multiple_of(piece * PIECE + first, 16), size)

    z_up, z_down, z_far = (z + 1) % 4, (z + 3) % 4, (z + 2) % 4
    flip = (core + turned) % 2
    window = pl.ds(pl.multiple_of(flip * (NVIR - WINDOW), 128), WINDOW)

    def at(chunk):
        job, begin, size = CHUNKS[chunk]
        return job, pl.ds(begin, size)

    def full(chunk, lines):
        job, w = at(chunk)
        if job == 4:
            return half_whole.at[lines, window]
        return whole.at[job, lines, w]

    def turn(slot, index):
        def body(step, carry):
            lines = pl.ds(pl.multiple_of(step * 128, 128), 128)
            flipped[index, :, lines] = jnp.transpose(rows[slot, lines, :].astype(jnp.float32)).astype(jnp.bfloat16)
            return carry

        lax.fori_loop(0, 2 * ROWS // 128, body, 0)

    flip_index = (0, 0, 1, 1, 2)
    arrived = set()

    def need(*names):
        for name in names:
            if name not in arrived:
                arrived.add(name)
                copies[name].wait_recv()

    def own():
        copies["own"].wait_recv()
        turn(OWN, 0)

    def next_a():
        copies["next a"].wait_recv()
        copies["next a on"] = pass_on(NEXT, first, 6)
        pl.when(lo == 0)(copies["mate a"].start)

    def next_b():
        copies["next b"].wait_recv()
        copies["next b on"] = pass_on(NEXT, second, 7)
        pl.when(lo == 0)(copies["mate b"].start)

    def prev():
        copies["prev"].wait_recv()
        copies["prev on"] = pass_on(PREV, everything, 8)

    def turn_prev():
        need("prev on")
        turn(PREV, 2)

    def mate():
        copies["mate a"].wait_recv()
        copies["mate b"].wait_recv()
        copies["mate on"] = pass_on(MATE, everything, 9)

    def turn_mate():
        copies["mate on"].wait_recv()
        turn(MATE, 1)

    def stage0(chunk):
        job, w = at(chunk)
        if job in (1, 4):
            need("next a on")
            if job == 4 or w.start + w.size > SPLIT:
                need("next b on")
        if job == 3:
            need("prev on")
        lhs = flipped[flip_index[job], pl.ds(pl.multiple_of(core * HALF, 16), HALF), :]
        rhs = rows[right[job], :, window] if job == 4 else rows[right[job], :, w]
        partial[job, :, w] = jnp.dot(lhs, rhs, preferred_element_type=jnp.float32).astype(jnp.bfloat16)
        copies[chunk, 0] = start(
            partial.at[job, part(z_far, 0, CUT), w], z1_up.at[job, :, w],
            send.at[chunk, 0], recv.at[chunk, 0], up,
        )
        copies[chunk, 1] = start(
            partial.at[job, part(z_far, CUT, PIECE - CUT), w], z1_down.at[job, :, w],
            send.at[chunk, 1], recv.at[chunk, 1], down,
        )

    def add(job, w, where, arrived):
        partial[job, where, w] = (
            partial[job, where, w].astype(jnp.float32) + arrived[job, :, w].astype(jnp.float32)
        ).astype(jnp.bfloat16)

    def stage1(chunk):
        job, w = at(chunk)
        copies[chunk, 0].wait_recv()
        add(job, w, part(z_up, 0, CUT), z1_up)
        copies[chunk, 2] = start(
            partial.at[job, part(z_up), w], z2_up.at[job, :, w], send.at[chunk, 2], recv.at[chunk, 2], up
        )
        copies[chunk, 1].wait_recv()
        add(job, w, part(z_down, CUT, PIECE - CUT), z1_down)
        copies[chunk, 3] = start(
            partial.at[job, part(z_down), w], z2_down.at[job, :, w], send.at[chunk, 3], recv.at[chunk, 3], down
        )

    def stage2(chunk):
        job, w = at(chunk)
        copies[chunk, 2].wait_recv()
        copies[chunk, 3].wait_recv()
        mine[job, :, w] = (
            partial[job, part(z), w].astype(jnp.float32)
            + z2_up[job, :, w].astype(jnp.float32)
            + z2_down[job, :, w].astype(jnp.float32)
        ).astype(jnp.bfloat16)
        copies[chunk, 4] = start(
            mine.at[job, :, w], other.at[job, :, w], send.at[chunk, 4], recv.at[chunk, 4], far
        )

    def same(chunk, lines, index, device):
        copies[chunk, index] = start(
            full(chunk, lines), full(chunk, lines), send.at[chunk, index], recv.at[chunk, index], device
        )

    def stage3(chunk):
        job, w = at(chunk)
        copies[chunk, 4].wait_recv()
        total = (mine[job, :, w].astype(jnp.float32) + other[job, :, w].astype(jnp.float32)).astype(jnp.bfloat16)
        if job == 4:
            half_whole[span(core, z), window] = total
        else:
            whole[job, span(core, z), w] = total
        same(chunk, span(core, z), 5, up)
        same(chunk, span(core, z), 6, down)
        same(chunk, span(core, z), 7, sibling)

    def stage4(chunk):
        copies[chunk, 5].wait_recv()
        same(chunk, span(core, z_down, 0, CUT), 8, up)
        same(chunk, span(core, z_down), 9, sibling)
        copies[chunk, 6].wait_recv()
        same(chunk, span(core, z_up, CUT, PIECE - CUT), 10, down)
        same(chunk, span(core, z_up), 11, sibling)

    def stage5(chunk):
        copies[chunk, 8].wait_recv()
        copies[chunk, 10].wait_recv()
        same(chunk, span(core, z_far), 12, sibling)

    def stage6(job):
        for chunk in range(len(CHUNKS)):
            if CHUNKS[chunk][0] == job:
                for index in (7, 9, 11, 12):
                    copies[chunk, index].wait_recv()
        source = half_whole if job == 4 else whole.at[job]
        base = pair_energy[job]

        def body(step, carry):
            lines = pl.ds(pl.multiple_of(step * 128, 128), 128)
            plain = source[lines, :].astype(jnp.float32)
            swapped = jnp.transpose(source[:, lines].astype(jnp.float32))
            gap = (base - virc[lines, 0:1]) - vir[...]
            value = (2.0 * plain - swapped) / gap
            if job == 4:
                a = lax.broadcasted_iota(jnp.int32, (128, NVIR), 0) + step * 128
                b = lax.broadcasted_iota(jnp.int32, (128, NVIR), 1)
                crossed = (a >= HALF).astype(jnp.int32) + (b >= HALF).astype(jnp.int32)
                value = jnp.where((crossed + turned) % 2 == 0, value, 0.0)
            amp[lines, :] = value.astype(jnp.bfloat16)
            return carry

        lax.fori_loop(0, NVIR // 128, body, 0)
        acc[left[job]] = acc[left[job]] + lax.dot_general(
            rows[right[job], own_part, :], amp[...], (((1,), (1,)), ((), ())), preferred_element_type=jnp.float32
        )
        if job > 0:
            acc[right[job]] = acc[right[job]] + jnp.dot(
                rows[left[job], own_part, :], amp[...], preferred_element_type=jnp.float32
            )

    def give_back(slot, device):
        index = slot - 1
        back_out[index] = acc[slot].astype(jnp.bfloat16)
        copies[slot] = start(
            back_out.at[index], back_in.at[index], b_send.at[10 + index], b_recv.at[10 + index], device
        )

    own()
    stage0(0)
    stage1(0)
    next_a()
    next_b()
    prev()
    stage0(1)
    turn_prev()
    stage0(4)
    stage1(1)
    stage1(4)
    mate()
    turn_mate()
    stage0(3)
    stage2(0)
    stage0(2)
    stage2(1)
    stage1(3)
    stage2(4)
    stage1(2)
    stage2(3)
    stage3(1)
    stage3(4)
    stage2(2)
    stage4(1)
    stage4(4)
    stage3(3)
    stage5(1)
    stage3(2)
    stage5(4)
    stage6(1)
    stage4(3)
    stage6(4)
    give_back(NEXT, above)
    stage4(2)
    stage3(0)
    stage5(3)
    stage5(2)
    stage6(3)
    stage6(2)
    give_back(MATE, giver)
    stage4(0)
    give_back(PREV, below)
    stage5(0)
    stage6(0)
    for slot in (NEXT, PREV, MATE):
        copies[slot].wait_recv()
    total = acc[OWN] + back_in[0].astype(jnp.float32)
    total = total + back_in[1].astype(jnp.float32) + back_in[2].astype(jnp.float32)
    out[...] = total.astype(jnp.bfloat16)
    for copy in started:
        copy.wait_send()


def on_device(b_rows, aux_count, occ_pick, eps_occ, eps_vir):
    bf16, f32 = jnp.bfloat16, jnp.float32
    smem, vmem = pl.BlockSpec(memory_space=pltpu.SMEM), pl.BlockSpec(memory_space=pltpu.VMEM)
    dma = pltpu.SemaphoreType.DMA
    gamma = pl.pallas_call(
        kernel,
        out_shape=jax.ShapeDtypeStruct((ROWS, NVIR), bf16),
        in_specs=[smem, smem, smem, vmem, vmem],
        out_specs=vmem,
        scratch_shapes=[
            pltpu.VMEM((4, 2 * ROWS, NVIR), bf16),
            pltpu.VMEM((3, NVIR, 2 * ROWS), bf16),
            pltpu.VMEM((4, ROWS, NVIR), f32),
            pltpu.VMEM((NVIR, NVIR), bf16),
            pltpu.VMEM((NVIR, 128), f32),
            pltpu.VMEM((JOBS, HALF, NVIR), bf16),
            pltpu.VMEM((JOBS - 1, NVIR, NVIR), bf16),
            pltpu.VMEM((NVIR, NVIR), bf16),
            pltpu.VMEM((JOBS, CUT, NVIR), bf16),
            pltpu.VMEM((JOBS, PIECE - CUT, NVIR), bf16),
            pltpu.VMEM((JOBS, PIECE, NVIR), bf16),
            pltpu.VMEM((JOBS, PIECE, NVIR), bf16),
            pltpu.VMEM((JOBS, PIECE, NVIR), bf16),
            pltpu.VMEM((JOBS, PIECE, NVIR), bf16),
            pltpu.VMEM((3, ROWS, NVIR), bf16),
            pltpu.VMEM((3, ROWS, NVIR), bf16),
            dma((len(CHUNKS), 13)), dma((len(CHUNKS), 13)), dma((13,)), dma((13,)),
        ],
        compiler_params=pltpu.CompilerParams(
            collective_id=0, has_side_effects=True, vmem_limit_bytes=56 * 2**20
        ),
    )(aux_count, occ_pick, eps_occ, eps_vir.reshape(1, NVIR), b_rows[:, 0, :])
    return gamma[:, None, :]


def solution(mesh):
    placed = (P("grp", "blk", None), P("grp"), P(), P(), P())
    return jax.shard_map(
        on_device, mesh=mesh, in_specs=placed, out_specs=P("grp", "blk", None), check_vma=False
    )
```

time: 123 us -> 103 us (0.84)
  Pallas kernels: 119 us -> 99.3 us
    pallas_call x1, Pallas kernels: 119 us -> 99.3 us  [on_device(): pl.pallas_call(kernel, out_shape=jax.ShapeDtypeStruct((ROWS, NVIR), bf16)...]
where the time goes in v2:
time: 103 us
  Pallas kernels  99.3 us (96%)
  local copies, waits for them, and re-layouts  3.18 us (3%)
    pallas_call x1, Pallas kernels, on_device(): pl.pallas_call(kernel, out_shape=jax.ShapeDtypeStruct((ROWS, NVIR), bf16)...  99.3 us

profile of v2, /device:TPU:1, one launch (start us, length us, event | category | flops | bytes accessed | tf_op | source)
XLA Modules:
  0.0 103.1 jit_solution(11504330356788423433)
XLA Ops:
  0.7 1.3 %reshape.3.vir = f32[1,896]{1,0:T(1,128)} reshape(f32[896]{0:T(1024)} %param.9) | data formatting | bytes 7168 | tf_op jit(solution)/shard_map/reshape | solution.py:392
  1.9 99.3 %shard_map.55 = bf16[320,896]{1,0:T(8,128)(2,1)} custom-call(s32[1]{0:T(128)S(6)} %copy.7.count, s32[8]{0:T(128)} %pick.1, f32[100]{0:T(128)} %occ.1, f32[1,896]{1,0:T(1,128)} %reshape.3.vir, bf16[320,896]{1,0:T(8,128)(2,1)} %bitcast.3), custom_call_target="tpu_custom_call" | custom-call | tf_op jit(solution)/shard_map/pallas_call | solution.py:365
  101.2 1.9 %copy.8 = bf16[320,1,896]{2,0,1:T(8,128)(2,1)} copy(bf16[320,1,896]{2,0,1:T(8,128)(2,1)} %bitcast.2) | data formatting | bytes 1146880

commit v3 on v2

--- a/solution.py
+++ b/solution.py
@@ -14,7 +14,7 @@
 WINDOW = 512
 OWN, NEXT, PREV, MATE = range(4)
 JOBS = 5
-CHUNKS = ((0, 0, 896), (1, 0, 896), (2, 0, 896), (3, 0, 896), (4, 0, 512))
+CHUNKS = ((0, 0, 512), (0, 512, 384), (1, 0, 512), (1, 512, 384), (2, 0, 512), (2, 512, 384), (3, 0, 512), (3, 512, 384), (4, 0, 512))
 
 
 def device_at(x, y, z, core):
@@ -308,45 +308,69 @@
     stage0(0)
     stage1(0)
     next_a()
+    stage0(1)
+    stage0(2)
+    stage1(1)
     next_b()
+    stage1(2)
     prev()
-    stage0(1)
+    stage0(3)
     turn_prev()
+    stage0(8)
+    stage2(2)
+    stage1(3)
+    stage1(8)
+    mate()
+    stage3(2)
+    turn_mate()
     stage0(4)
-    stage1(1)
+    stage2(3)
+    stage0(6)
+    stage2(8)
+    stage0(5)
+    stage4(2)
+    stage0(7)
+    stage1(5)
     stage1(4)
-    mate()
-    turn_mate()
-    stage0(3)
+    stage3(8)
+    stage3(3)
+    stage2(4)
+    stage1(6)
+    stage2(5)
+    stage4(3)
+    stage4(8)
+    stage1(7)
+    stage2(6)
+    stage3(5)
+    stage5(2)
+    stage5(3)
+    stage3(4)
+    stage5(8)
     stage2(0)
-    stage0(2)
+    stage6(1)
+    stage2(7)
+    stage4(5)
+    stage3(6)
+    stage6(4)
+    stage4(4)
+    stage3(7)
+    give_back(NEXT, above)
     stage2(1)
-    stage1(3)
-    stage2(4)
-    stage1(2)
-    stage2(3)
+    stage5(5)
+    stage5(4)
+    stage4(6)
+    stage4(7)
+    stage6(2)
+    stage5(6)
+    stage5(7)
     stage3(1)
-    stage3(4)
-    stage2(2)
+    stage6(3)
+    give_back(MATE, giver)
+    give_back(PREV, below)
+    stage3(0)
     stage4(1)
-    stage4(4)
-    stage3(3)
     stage5(1)
-    stage3(2)
-    stage5(4)
-    stage6(1)
-    stage4(3)
-    stage6(4)
-    give_back(NEXT, above)
-    stage4(2)
-    stage3(0)
-    stage5(3)
-    stage5(2)
-    stage6(3)
-    stage6(2)
-    give_back(MATE, giver)
     stage4(0)
-    give_back(PREV, below)
     stage5(0)
     stage6(0)
     for slot in (NEXT, PREV, MATE):

time: 103 us -> 104 us (level)
  no operation moved by 1% of the time
where the time goes in v3:
time: 104 us; the launch traced here: 103 us
  Pallas kernels  99.5 us (96%)
  local copies, waits for them, and re-layouts  3.18 us (3%)
    pallas_call x1, Pallas kernels, on_device(): pl.pallas_call(kernel, out_shape=jax.ShapeDtypeStruct((ROWS, NVIR), bf16)...  99.5 us

profile of v3, /device:TPU:1, one launch (start us, length us, event | category | flops | bytes accessed | tf_op | source)
XLA Modules:
  0.0 103.4 jit_solution(11023901036397529070)
XLA Ops:
  0.7 1.3 %reshape.3.vir = f32[1,896]{1,0:T(1,128)} reshape(f32[896]{0:T(1024)} %param.9) | data formatting | bytes 7168 | tf_op jit(solution)/shard_map/reshape | solution.py:416
  1.9 99.5 %shard_map.55 = bf16[320,896]{1,0:T(8,128)(2,1)} custom-call(s32[1]{0:T(128)S(6)} %copy.7.count, s32[8]{0:T(128)} %pick.1, f32[100]{0:T(128)} %occ.1, f32[1,896]{1,0:T(1,128)} %reshape.3.vir, bf16[320,896]{1,0:T(8,128)(2,1)} %bitcast.3), custom_call_target="tpu_custom_call" | custom-call | tf_op jit(solution)/shard_map/pallas_call | solution.py:389
  101.4 1.9 %copy.8 = bf16[320,1,896]{2,0,1:T(8,128)(2,1)} copy(bf16[320,1,896]{2,0,1:T(8,128)(2,1)} %bitcast.2) | data formatting | bytes 1146880

commit v4 on v3

--- a/solution.py
+++ b/solution.py
@@ -9,12 +9,13 @@
 ROWS, NVIR = 320, 896
 HALF = NVIR // 2
 PIECE = HALF // 4
-CUT = 64
+CUTS = (64, 48)
 SPLIT = 512
 WINDOW = 512
 OWN, NEXT, PREV, MATE = range(4)
 JOBS = 5
 CHUNKS = ((0, 0, 512), (0, 512, 384), (1, 0, 512), (1, 512, 384), (2, 0, 512), (2, 512, 384), (3, 0, 512), (3, 512, 384), (4, 0, 512))
+TURNS = (1, 0, 0, 1, 1, 0, 1, 0, 0)
 
 
 def device_at(x, y, z, core):
@@ -22,8 +23,9 @@
 
 
 def kernel(
-    count, pick, occ, vir, b_ref, out,
-    rows, flipped, acc, amp, virc, partial, whole, half_whole,
+    count_ref, pick_ref, occ_ref, vir, b_ref, out,
+    count, pick, occ, small,
+    rows, flipped, acc, amp, virc, virr, partial, whole, half_whole,
     z1_up, z1_down, z2_up, z2_down, mine, other, back_out, back_in,
     send, recv, b_send, b_recv,
 ):
@@ -57,15 +59,31 @@
         copy.start()
         return copy
 
-    line = lax.broadcasted_iota(jnp.int32, (ROWS, NVIR), 0)
-    live = jnp.where(line < count[0], b_ref[...].astype(jnp.float32), 0.0).astype(jnp.bfloat16)
-    rows[OWN, own_part, :] = live
+    fetches = [
+        pltpu.make_async_copy(src, dst, small.at[index])
+        for index, (src, dst) in enumerate(
+            ((b_ref, rows.at[OWN, own_part]), (count_ref, count), (pick_ref, pick), (occ_ref, occ))
+        )
+    ]
+    for fetch in fetches:
+        fetch.start()
     half_whole[...] = jnp.zeros_like(half_whole)
 
     barrier = pltpu.get_barrier_semaphore()
     everyone = (sibling, above, below, partner, diagonal, far, up, down)
     for device in everyone:
         pl.semaphore_signal(barrier, inc=1, device_id=device, device_id_type=MESH)
+
+    acc[...] = jnp.zeros_like(acc)
+    virc[...] = jnp.transpose(jnp.broadcast_to(vir[...].reshape(1, NVIR), (128, NVIR)))
+    virr[...] = jnp.broadcast_to(vir[...].reshape(1, NVIR), (8, NVIR))
+
+    for fetch in fetches:
+        fetch.wait()
+    line = lax.broadcasted_iota(jnp.int32, (ROWS, NVIR), 0)
+    live = jnp.where(line < count[0], rows[OWN, own_part, :].astype(jnp.float32), 0.0)
+    rows[OWN, own_part, :] = live.astype(jnp.bfloat16)
+
     pl.semaphore_wait(barrier, len(everyone))
 
     first, second = pl.ds(0, SPLIT), pl.ds(SPLIT, NVIR - SPLIT)
@@ -101,9 +119,6 @@
     def _():
         copies["mate a"].start()
         copies["mate b"].start()
-
-    acc[...] = jnp.zeros_like(acc)
-    virc[...] = jnp.transpose(jnp.broadcast_to(vir[...], (128, NVIR)))
 
     def energy(position):
         return occ[pick[position]]
@@ -130,6 +145,9 @@
     def at(chunk):
         job, begin, size = CHUNKS[chunk]
         return job, pl.ds(begin, size)
+
+    def cut(chunk):
+        return CUTS[TURNS[chunk]]
 
     def full(chunk, lines):
         job, w = at(chunk)
@@ -197,28 +215,30 @@
         rhs = rows[right[job], :, window] if job == 4 else rows[right[job], :, w]
         partial[job, :, w] = jnp.dot(lhs, rhs, preferred_element_type=jnp.float32).astype(jnp.bfloat16)
         copies[chunk, 0] = start(
-            partial.at[job, part(z_far, 0, CUT), w], z1_up.at[job, :, w],
+            partial.at[job, part(z_far, 0, cut(chunk)), w], z1_up.at[job, pl.ds(0, cut(chunk)), w],
             send.at[chunk, 0], recv.at[chunk, 0], up,
         )
         copies[chunk, 1] = start(
-            partial.at[job, part(z_far, CUT, PIECE - CUT), w], z1_down.at[job, :, w],
+            partial.at[job, part(z_far, cut(chunk), PIECE - cut(chunk)), w],
+            z1_down.at[job, pl.ds(0, PIECE - cut(chunk)), w],
             send.at[chunk, 1], recv.at[chunk, 1], down,
         )
 
-    def add(job, w, where, arrived):
+    def add(job, w, piece, begin, size, arrived):
+        where = part(piece, begin, size)
         partial[job, where, w] = (
-            partial[job, where, w].astype(jnp.float32) + arrived[job, :, w].astype(jnp.float32)
+            partial[job, where, w].astype(jnp.float32) + arrived[job, 0:size, w].astype(jnp.float32)
         ).astype(jnp.bfloat16)
 
     def stage1(chunk):
         job, w = at(chunk)
         copies[chunk, 0].wait_recv()
-        add(job, w, part(z_up, 0, CUT), z1_up)
+        add(job, w, z_up, 0, cut(chunk), z1_up)
         copies[chunk, 2] = start(
             partial.at[job, part(z_up), w], z2_up.at[job, :, w], send.at[chunk, 2], recv.at[chunk, 2], up
         )
         copies[chunk, 1].wait_recv()
-        add(job, w, part(z_down, CUT, PIECE - CUT), z1_down)
+        add(job, w, z_down, cut(chunk), PIECE - cut(chunk), z1_down)
         copies[chunk, 3] = start(
             partial.at[job, part(z_down), w], z2_down.at[job, :, w], send.at[chunk, 3], recv.at[chunk, 3], down
         )
@@ -255,10 +275,10 @@
 
     def stage4(chunk):
         copies[chunk, 5].wait_recv()
-        same(chunk, span(core, z_down, 0, CUT), 8, up)
+        same(chunk, span(core, z_down, 0, cut(chunk)), 8, up)
         same(chunk, span(core, z_down), 9, sibling)
         copies[chunk, 6].wait_recv()
-        same(chunk, span(core, z_up, CUT, PIECE - CUT), 10, down)
+        same(chunk, span(core, z_up, cut(chunk), PIECE - cut(chunk)), 10, down)
         same(chunk, span(core, z_up), 11, sibling)
 
     def stage5(chunk):
@@ -278,23 +298,32 @@
             lines = pl.ds(pl.multiple_of(step * 128, 128), 128)
             plain = source[lines, :].astype(jnp.float32)
             swapped = jnp.transpose(source[:, lines].astype(jnp.float32))
-            gap = (base - virc[lines, 0:1]) - vir[...]
+            gap = (base - virc[lines, 0:1]) - virr[0:1, :]
             value = (2.0 * plain - swapped) / gap
             if job == 4:
                 a = lax.broadcasted_iota(jnp.int32, (128, NVIR), 0) + step * 128
                 b = lax.broadcasted_iota(jnp.int32, (128, NVIR), 1)
                 crossed = (a >= HALF).astype(jnp.int32) + (b >= HALF).astype(jnp.int32)
                 value = jnp.where((crossed + turned) % 2 == 0, value, 0.0)
-            amp[lines, :] = value.astype(jnp.bfloat16)
+            amp[job, lines, :] = value.astype(jnp.bfloat16)
             return carry
 
         lax.fori_loop(0, NVIR // 128, body, 0)
-        acc[left[job]] = acc[left[job]] + lax.dot_general(
-            rows[right[job], own_part, :], amp[...], (((1,), (1,)), ((), ())), preferred_element_type=jnp.float32
-        )
-        if job > 0:
+        apply(job, first_side[job])
+
+    def stage8(job):
+        apply(job, 1 - first_side[job])
+
+    first_side = (0, 1, 0, 0, 1)
+
+    def apply(job, side):
+        if side == 0:
+            acc[left[job]] = acc[left[job]] + lax.dot_general(
+                rows[right[job], own_part, :], amp[job], (((1,), (1,)), ((), ())), preferred_element_type=jnp.float32
+            )
+        else:
             acc[right[job]] = acc[right[job]] + jnp.dot(
-                rows[left[job], own_part, :], amp[...], preferred_element_type=jnp.float32
+                rows[left[job], own_part, :], amp[job], preferred_element_type=jnp.float32
             )
 
     def give_back(slot, device):
@@ -306,17 +335,17 @@
 
     own()
     stage0(0)
+    stage0(1)
+    next_a()
+    stage0(2)
     stage1(0)
-    next_a()
-    stage0(1)
-    stage0(2)
-    stage1(1)
+    prev()
     next_b()
     stage1(2)
-    prev()
+    turn_prev()
     stage0(3)
-    turn_prev()
     stage0(8)
+    stage1(1)
     stage2(2)
     stage1(3)
     stage1(8)
@@ -324,55 +353,59 @@
     stage3(2)
     turn_mate()
     stage0(4)
-    stage2(3)
+    stage0(5)
+    stage0(7)
+    stage2(8)
     stage0(6)
-    stage2(8)
-    stage0(5)
-    stage4(2)
-    stage0(7)
-    stage1(5)
     stage1(4)
     stage3(8)
+    stage1(6)
+    stage1(7)
+    stage2(3)
+    stage2(4)
+    stage4(8)
     stage3(3)
-    stage2(4)
-    stage1(6)
-    stage2(5)
+    stage1(5)
+    stage2(6)
+    stage2(7)
+    stage4(2)
+    stage2(1)
+    stage2(0)
+    stage5(8)
     stage4(3)
-    stage4(8)
-    stage1(7)
-    stage2(6)
-    stage3(5)
-    stage5(2)
-    stage5(3)
-    stage3(4)
-    stage5(8)
-    stage2(0)
-    stage6(1)
-    stage2(7)
-    stage4(5)
     stage3(6)
     stage6(4)
+    stage2(5)
+    stage3(7)
+    stage8(4)
+    stage5(3)
+    stage5(2)
+    stage3(4)
+    stage4(6)
+    stage6(1)
+    give_back(NEXT, above)
+    stage4(7)
+    stage3(5)
+    stage5(6)
     stage4(4)
-    stage3(7)
-    give_back(NEXT, above)
-    stage2(1)
+    stage5(7)
+    stage8(1)
+    stage4(5)
+    stage6(3)
+    stage3(1)
+    stage5(4)
     stage5(5)
-    stage5(4)
-    stage4(6)
-    stage4(7)
+    stage3(0)
+    stage8(3)
     stage6(2)
-    stage5(6)
-    stage5(7)
-    stage3(1)
-    stage6(3)
     give_back(MATE, giver)
     give_back(PREV, below)
-    stage3(0)
+    stage4(0)
     stage4(1)
+    stage5(0)
     stage5(1)
-    stage4(0)
-    stage5(0)
     stage6(0)
+    stage8(2)
     for slot in (NEXT, PREV, MATE):
         copies[slot].wait_recv()
     total = acc[OWN] + back_in[0].astype(jnp.float32)
@@ -384,24 +417,29 @@
 
 def on_device(b_rows, aux_count, occ_pick, eps_occ, eps_vir):
     bf16, f32 = jnp.bfloat16, jnp.float32
-    smem, vmem = pl.BlockSpec(memory_space=pltpu.SMEM), pl.BlockSpec(memory_space=pltpu.VMEM)
+    hbm, vmem = pl.BlockSpec(memory_space=pl.ANY), pl.BlockSpec(memory_space=pltpu.VMEM)
     dma = pltpu.SemaphoreType.DMA
     gamma = pl.pallas_call(
         kernel,
         out_shape=jax.ShapeDtypeStruct((ROWS, NVIR), bf16),
-        in_specs=[smem, smem, smem, vmem, vmem],
+        in_specs=[hbm, hbm, hbm, vmem, hbm],
         out_specs=vmem,
         scratch_shapes=[
+            pltpu.SMEM((1,), jnp.int32),
+            pltpu.SMEM((8,), jnp.int32),
+            pltpu.SMEM((100,), f32),
+            dma((4,)),
             pltpu.VMEM((4, 2 * ROWS, NVIR), bf16),
             pltpu.VMEM((3, NVIR, 2 * ROWS), bf16),
             pltpu.VMEM((4, ROWS, NVIR), f32),
-            pltpu.VMEM((NVIR, NVIR), bf16),
+            pltpu.VMEM((JOBS, NVIR, NVIR), bf16),
             pltpu.VMEM((NVIR, 128), f32),
+            pltpu.VMEM((8, NVIR), f32),
             pltpu.VMEM((JOBS, HALF, NVIR), bf16),
             pltpu.VMEM((JOBS - 1, NVIR, NVIR), bf16),
             pltpu.VMEM((NVIR, NVIR), bf16),
-            pltpu.VMEM((JOBS, CUT, NVIR), bf16),
-            pltpu.VMEM((JOBS, PIECE - CUT, NVIR), bf16),
+            pltpu.VMEM((JOBS, max(CUTS), NVIR), bf16),
+            pltpu.VMEM((JOBS, max(CUTS), NVIR), bf16),
             pltpu.VMEM((JOBS, PIECE, NVIR), bf16),
             pltpu.VMEM((JOBS, PIECE, NVIR), bf16),
             pltpu.VMEM((JOBS, PIECE, NVIR), bf16),
@@ -413,7 +451,7 @@
         compiler_params=pltpu.CompilerParams(
             collective_id=0, has_side_effects=True, vmem_limit_bytes=56 * 2**20
         ),
-    )(aux_count, occ_pick, eps_occ, eps_vir.reshape(1, NVIR), b_rows[:, 0, :])
+    )(aux_count, occ_pick, eps_occ, eps_vir, b_rows[:, 0, :])
     return gamma[:, None, :]
 
 

time: 104 us -> 98.6 us (0.948)
  Pallas kernels: 99.5 us -> 95.9 us
  local copies, waits for them, and re-layouts: 3.18 us -> 1.91 us
    pallas_call x1, Pallas kernels: 99.5 us -> 95.9 us  [on_device(): pl.pallas_call(kernel, out_shape=jax.ShapeDtypeStruct((ROWS, NVIR), bf16)...]
    reshape x1 -> x0, local copies, waits for them, and re-layouts: 1.27 us -> none  [on_device(): eps_vir.reshape(1, NVIR)]
where the time goes in v4:
time: 98.6 us; the launch traced here: 98.4 us
  Pallas kernels  95.9 us (97%)
  local copies, waits for them, and re-layouts  1.91 us (2%)
    pallas_call x1, Pallas kernels, on_device(): pl.pallas_call(kernel, out_shape=jax.ShapeDtypeStruct((ROWS, NVIR), bf16)...  95.9 us

profile of v4, /device:TPU:1, one launch (start us, length us, event | category | flops | bytes accessed | tf_op | source)
XLA Modules:
  0.0 98.4 jit_solution(18154347318566681214)
XLA Ops:
  0.7 95.9 %shard_map.55 = bf16[320,896]{1,0:T(8,128)(2,1)} custom-call(s32[1]{0:T(128)S(6)} %copy.7.count_ref, s32[8]{0:T(128)} %pick_ref.1, f32[100]{0:T(128)} %occ_ref.1, f32[896]{0:T(1024)} %vir.1, bf16[320,896]{1,0:T(8,128)(2,1)} %bitcast.3), custom_call_target="tpu_custom_call" | custom-call | tf_op jit(solution)/shard_map/pallas_call | solution.py:422
  96.5 1.9 %copy.8 = bf16[320,1,896]{2,0,1:T(8,128)(2,1)} copy(bf16[320,1,896]{2,0,1:T(8,128)(2,1)} %bitcast.2) | data formatting | bytes 1146880

commit v5 on v4

--- a/solution.py
+++ b/solution.py
@@ -158,10 +158,10 @@
     def turn(slot, index):
         def body(step, carry):
             lines = pl.ds(pl.multiple_of(step * 128, 128), 128)
-            flipped[index, :, lines] = jnp.transpose(rows[slot, lines, :].astype(jnp.float32)).astype(jnp.bfloat16)
+            flipped[index, :, lines] = jnp.transpose(rows[slot, lines, :])
             return carry
 
-        lax.fori_loop(0, 2 * ROWS // 128, body, 0)
+        lax.fori_loop(0, 2 * ROWS // 128, body, 0, unroll=True)
 
     flip_index = (0, 0, 1, 1, 2)
     arrived = set()
@@ -297,7 +297,7 @@
         def body(step, carry):
             lines = pl.ds(pl.multiple_of(step * 128, 128), 128)
             plain = source[lines, :].astype(jnp.float32)
-            swapped = jnp.transpose(source[:, lines].astype(jnp.float32))
+            swapped = jnp.transpose(source[:, lines]).astype(jnp.float32)
             gap = (base - virc[lines, 0:1]) - virr[0:1, :]
             value = (2.0 * plain - swapped) / gap
             if job == 4:
@@ -308,7 +308,7 @@
             amp[job, lines, :] = value.astype(jnp.bfloat16)
             return carry
 
-        lax.fori_loop(0, NVIR // 128, body, 0)
+        lax.fori_loop(0, NVIR // 128, body, 0, unroll=True)
         apply(job, first_side[job])
 
     def stage8(job):
@@ -334,78 +334,78 @@
         )
 
     own()
+    stage0(1)
+    stage1(1)
     stage0(0)
-    stage0(1)
     next_a()
     stage0(2)
     stage1(0)
-    prev()
     next_b()
     stage1(2)
+    prev()
+    stage0(3)
     turn_prev()
-    stage0(3)
     stage0(8)
-    stage1(1)
     stage2(2)
     stage1(3)
     stage1(8)
     mate()
+    stage2(3)
     stage3(2)
     turn_mate()
+    stage2(8)
+    stage0(6)
     stage0(4)
+    stage2(0)
+    stage3(3)
+    stage4(2)
     stage0(5)
     stage0(7)
-    stage2(8)
-    stage0(6)
+    stage1(6)
     stage1(4)
-    stage3(8)
-    stage1(6)
-    stage1(7)
-    stage2(3)
-    stage2(4)
-    stage4(8)
-    stage3(3)
     stage1(5)
     stage2(6)
+    stage3(8)
+    stage2(4)
+    stage1(7)
+    stage4(3)
+    stage4(8)
+    stage5(2)
+    stage2(5)
+    stage3(4)
     stage2(7)
-    stage4(2)
+    stage5(3)
+    stage3(6)
+    stage5(8)
+    stage6(1)
+    stage3(5)
+    stage6(4)
+    give_back(NEXT, above)
+    stage3(7)
     stage2(1)
-    stage2(0)
-    stage5(8)
-    stage4(3)
-    stage3(6)
-    stage6(4)
-    stage2(5)
-    stage3(7)
+    stage4(4)
+    stage4(5)
+    stage4(6)
+    stage4(7)
     stage8(4)
-    stage5(3)
-    stage5(2)
-    stage3(4)
-    stage4(6)
-    stage6(1)
-    give_back(NEXT, above)
-    stage4(7)
-    stage3(5)
+    stage5(4)
+    stage3(1)
+    stage3(0)
+    stage5(5)
     stage5(6)
-    stage4(4)
     stage5(7)
+    stage6(2)
+    stage6(3)
+    give_back(MATE, giver)
+    stage8(3)
+    give_back(PREV, below)
+    stage4(1)
     stage8(1)
-    stage4(5)
-    stage6(3)
-    stage3(1)
-    stage5(4)
-    stage5(5)
-    stage3(0)
-    stage8(3)
-    stage6(2)
-    give_back(MATE, giver)
-    give_back(PREV, below)
+    stage8(2)
+    stage5(1)
     stage4(0)
-    stage4(1)
     stage5(0)
-    stage5(1)
     stage6(0)
-    stage8(2)
     for slot in (NEXT, PREV, MATE):
         copies[slot].wait_recv()
     total = acc[OWN] + back_in[0].astype(jnp.float32)

time: 98.6 us -> 96.5 us (0.979)
  Pallas kernels: 95.9 us -> 93.7 us
    pallas_call x1, Pallas kernels: 95.9 us -> 93.7 us  [on_device(): pl.pallas_call(kernel, out_shape=jax.ShapeDtypeStruct((ROWS, NVIR), bf16)...]
where the time goes in v5:
time: 96.5 us; the launch traced here: 96.3 us
  Pallas kernels  93.7 us (97%)
  local copies, waits for them, and re-layouts  1.91 us (2%)
    pallas_call x1, Pallas kernels, on_device(): pl.pallas_call(kernel, out_shape=jax.ShapeDtypeStruct((ROWS, NVIR), bf16)...  93.7 us

profile of v5, /device:TPU:1, one launch (start us, length us, event | category | flops | bytes accessed | tf_op | source)
XLA Modules:
  0.0 96.3 jit_solution(3121532712372290661)
XLA Ops:
  0.7 93.7 %shard_map.55 = bf16[320,896]{1,0:T(8,128)(2,1)} custom-call(s32[1]{0:T(128)S(6)} %copy.7.count_ref, s32[8]{0:T(128)} %pick_ref.1, f32[100]{0:T(128)} %occ_ref.1, f32[896]{0:T(1024)} %vir.1, bf16[320,896]{1,0:T(8,128)(2,1)} %bitcast.3), custom_call_target="tpu_custom_call" | custom-call | tf_op jit(solution)/shard_map/pallas_call | solution.py:422
  94.4 1.9 %copy.8 = bf16[320,1,896]{2,0,1:T(8,128)(2,1)} copy(bf16[320,1,896]{2,0,1:T(8,128)(2,1)} %bitcast.2) | data formatting | bytes 1146880

commit v6 on v5

--- a/solution.py
+++ b/solution.py
@@ -10,12 +10,13 @@
 HALF = NVIR // 2
 PIECE = HALF // 4
 CUTS = (64, 48)
-SPLIT = 512
+PARTS = ((0, 256), (256, 256), (512, 384))
 WINDOW = 512
 OWN, NEXT, PREV, MATE = range(4)
 JOBS = 5
-CHUNKS = ((0, 0, 512), (0, 512, 384), (1, 0, 512), (1, 512, 384), (2, 0, 512), (2, 512, 384), (3, 0, 512), (3, 512, 384), (4, 0, 512))
-TURNS = (1, 0, 0, 1, 1, 0, 1, 0, 0)
+CHUNKS = ((0, 0, 512), (0, 512, 384), (1, 0, 256), (1, 256, 256), (1, 512, 384), (2, 0, 512), (2, 512, 384), (3, 0, 512), (3, 512, 384), (4, 0, 512))
+TURNS = (0, 1, 0, 1, 0, 0, 1, 0, 1, 1)
+CROSSED = (5,)
 
 
 def device_at(x, y, z, core):
@@ -26,7 +27,7 @@
     count_ref, pick_ref, occ_ref, vir, b_ref, out,
     count, pick, occ, small,
     rows, flipped, acc, amp, virc, virr, partial, whole, half_whole,
-    z1_up, z1_down, z2_up, z2_down, mine, other, back_out, back_in,
+    z1_up, z1_down, z2_up, z2_down, mine, other, crossing, back_out, back_in,
     send, recv, b_send, b_recv,
 ):
     blk, grp = lax.axis_index("blk"), lax.axis_index("grp")
@@ -86,7 +87,6 @@
 
     pl.semaphore_wait(barrier, len(everyone))
 
-    first, second = pl.ds(0, SPLIT), pl.ds(SPLIT, NVIR - SPLIT)
     everything = pl.ds(0, NVIR)
 
     def spread(slot, columns, index, device):
@@ -108,17 +108,18 @@
         )
 
     copies = {}
+    pieces = range(len(PARTS))
     copies["own"] = spread(OWN, everything, 0, sibling)
-    copies["next a"] = spread(NEXT, first, 1, below)
-    copies["next b"] = spread(NEXT, second, 2, below)
-    copies["prev"] = spread(PREV, everything, 3, above)
-    copies["mate a"] = to_partner(first, 4)
-    copies["mate b"] = to_partner(second, 5)
+    for i in pieces:
+        copies["next", i] = spread(NEXT, pl.ds(*PARTS[i]), 7 + i, below)
+    copies["prev"] = spread(PREV, everything, 1, above)
+    for i in pieces:
+        copies["mate", i] = to_partner(pl.ds(*PARTS[i]), 13 + i)
 
     @pl.when(lo == 1)
     def _():
-        copies["mate a"].start()
-        copies["mate b"].start()
+        for i in pieces:
+            copies["mate", i].start()
 
     def energy(position):
         return occ[pick[position]]
@@ -142,17 +143,24 @@
     flip = (core + turned) % 2
     window = pl.ds(pl.multiple_of(flip * (NVIR - WINDOW), 128), WINDOW)
 
-    def at(chunk):
+    side = x // 2
+
+    def at(chunk, of=None):
         job, begin, size = CHUNKS[chunk]
-        return job, pl.ds(begin, size)
+        if chunk not in CROSSED:
+            return job, pl.ds(begin, size)
+        if of is None:
+            of = side
+        return job, pl.ds(pl.multiple_of(begin + of * (size // 2), 128), size // 2)
 
     def cut(chunk):
         return CUTS[TURNS[chunk]]
 
-    def full(chunk, lines):
-        job, w = at(chunk)
+    def full(chunk, lines, of=None):
+        job, w = at(chunk, of)
         if job == 4:
-            return half_whole.at[lines, window]
+            begin = pl.multiple_of(flip * (NVIR - WINDOW) + w.start, 128)
+            return half_whole.at[lines, pl.ds(begin, w.size)]
         return whole.at[job, lines, w]
 
     def turn(slot, index):
@@ -176,44 +184,58 @@
         copies["own"].wait_recv()
         turn(OWN, 0)
 
-    def next_a():
-        copies["next a"].wait_recv()
-        copies["next a on"] = pass_on(NEXT, first, 6)
-        pl.when(lo == 0)(copies["mate a"].start)
-
-    def next_b():
-        copies["next b"].wait_recv()
-        copies["next b on"] = pass_on(NEXT, second, 7)
-        pl.when(lo == 0)(copies["mate b"].start)
+    def next_part(i):
+        copies["next", i].wait_recv()
+        copies["next on", i] = pass_on(NEXT, pl.ds(*PARTS[i]), 10 + i)
+        pl.when(lo == 0)(copies["mate", i].start)
 
     def prev():
         copies["prev"].wait_recv()
-        copies["prev on"] = pass_on(PREV, everything, 8)
+        copies["prev on"] = pass_on(PREV, everything, 2)
 
     def turn_prev():
         need("prev on")
         turn(PREV, 2)
 
     def mate():
-        copies["mate a"].wait_recv()
-        copies["mate b"].wait_recv()
-        copies["mate on"] = pass_on(MATE, everything, 9)
+        for i in pieces:
+            copies["mate", i].wait_recv()
+        copies["mate on"] = pass_on(MATE, everything, 3)
 
     def turn_mate():
         copies["mate on"].wait_recv()
         turn(MATE, 1)
 
     def stage0(chunk):
-        job, w = at(chunk)
+        job, begin, size = CHUNKS[chunk]
+        w = pl.ds(begin, size)
         if job in (1, 4):
-            need("next a on")
-            if job == 4 or w.start + w.size > SPLIT:
-                need("next b on")
+            for i in pieces:
+                if job == 4 or PARTS[i][0] < begin + size:
+                    need(("next on", i))
         if job == 3:
             need("prev on")
         lhs = flipped[flip_index[job], pl.ds(pl.multiple_of(core * HALF, 16), HALF), :]
         rhs = rows[right[job], :, window] if job == 4 else rows[right[job], :, w]
         partial[job, :, w] = jnp.dot(lhs, rhs, preferred_element_type=jnp.float32).astype(jnp.bfloat16)
+        if chunk in CROSSED:
+            copies[chunk, 13] = start(
+                partial.at[job, :, at(chunk, 1 - side)[1]], crossing.at[CROSSED.index(chunk)],
+                send.at[chunk, 13], recv.at[chunk, 13], far,
+            )
+        else:
+            into_ring(chunk)
+
+    def stage9(chunk):
+        job, w = at(chunk)
+        copies[chunk, 13].wait_recv()
+        partial[job, :, w] = (
+            partial[job, :, w].astype(jnp.float32) + crossing[CROSSED.index(chunk)].astype(jnp.float32)
+        ).astype(jnp.bfloat16)
+        into_ring(chunk)
+
+    def into_ring(chunk):
+        job, w = at(chunk)
         copies[chunk, 0] = start(
             partial.at[job, part(z_far, 0, cut(chunk)), w], z1_up.at[job, pl.ds(0, cut(chunk)), w],
             send.at[chunk, 0], recv.at[chunk, 0], up,
@@ -243,54 +265,69 @@
             partial.at[job, part(z_down), w], z2_down.at[job, :, w], send.at[chunk, 3], recv.at[chunk, 3], down
         )
 
-    def stage2(chunk):
+    def ring_sum(chunk):
         job, w = at(chunk)
         copies[chunk, 2].wait_recv()
         copies[chunk, 3].wait_recv()
-        mine[job, :, w] = (
+        return (
             partial[job, part(z), w].astype(jnp.float32)
             + z2_up[job, :, w].astype(jnp.float32)
             + z2_down[job, :, w].astype(jnp.float32)
         ).astype(jnp.bfloat16)
+
+    def stage2(chunk):
+        job, w = at(chunk)
+        mine[job, :, w] = ring_sum(chunk)
         copies[chunk, 4] = start(
             mine.at[job, :, w], other.at[job, :, w], send.at[chunk, 4], recv.at[chunk, 4], far
         )
 
-    def same(chunk, lines, index, device):
+    def same(chunk, lines, index, device, of=None):
         copies[chunk, index] = start(
-            full(chunk, lines), full(chunk, lines), send.at[chunk, index], recv.at[chunk, index], device
-        )
+            full(chunk, lines, of), full(chunk, lines, of), send.at[chunk, index], recv.at[chunk, index], device
+        )
+
+    def both(chunk, lines, index):
+        same(chunk, lines, index, sibling)
+        if chunk in CROSSED:
+            same(chunk, lines, {7: 14, 9: 15, 11: 16, 12: 17}[index], far)
 
     def stage3(chunk):
         job, w = at(chunk)
-        copies[chunk, 4].wait_recv()
-        total = (mine[job, :, w].astype(jnp.float32) + other[job, :, w].astype(jnp.float32)).astype(jnp.bfloat16)
-        if job == 4:
-            half_whole[span(core, z), window] = total
+        if chunk in CROSSED:
+            total = ring_sum(chunk)
         else:
-            whole[job, span(core, z), w] = total
+            copies[chunk, 4].wait_recv()
+            total = mine[job, :, w].astype(jnp.float32) + other[job, :, w].astype(jnp.float32)
+        full(chunk, span(core, z))[...] = total.astype(jnp.bfloat16)
         same(chunk, span(core, z), 5, up)
         same(chunk, span(core, z), 6, down)
-        same(chunk, span(core, z), 7, sibling)
+        both(chunk, span(core, z), 7)
 
     def stage4(chunk):
         copies[chunk, 5].wait_recv()
         same(chunk, span(core, z_down, 0, cut(chunk)), 8, up)
-        same(chunk, span(core, z_down), 9, sibling)
+        both(chunk, span(core, z_down), 9)
         copies[chunk, 6].wait_recv()
         same(chunk, span(core, z_up, cut(chunk), PIECE - cut(chunk)), 10, down)
-        same(chunk, span(core, z_up), 11, sibling)
+        both(chunk, span(core, z_up), 11)
 
     def stage5(chunk):
         copies[chunk, 8].wait_recv()
         copies[chunk, 10].wait_recv()
-        same(chunk, span(core, z_far), 12, sibling)
+        both(chunk, span(core, z_far), 12)
+
+    def stage7(chunk):
+        for index in (14, 15, 16, 17):
+            copies[chunk, index].wait_recv()
+        same(chunk, pl.ds(pl.multiple_of(core * HALF, 16), HALF), 18, sibling, 1 - side)
 
     def stage6(job):
         for chunk in range(len(CHUNKS)):
             if CHUNKS[chunk][0] == job:
-                for index in (7, 9, 11, 12):
-                    copies[chunk, index].wait_recv()
+                for index in (7, 9, 11, 12, 18):
+                    if index < 18 or chunk in CROSSED:
+                        copies[chunk, index].wait_recv()
         source = half_whole if job == 4 else whole.at[job]
         base = pair_energy[job]
 
@@ -330,79 +367,87 @@
         index = slot - 1
         back_out[index] = acc[slot].astype(jnp.bfloat16)
         copies[slot] = start(
-            back_out.at[index], back_in.at[index], b_send.at[10 + index], b_recv.at[10 + index], device
+            back_out.at[index], back_in.at[index], b_send.at[4 + index], b_recv.at[4 + index], device
         )
 
     own()
     stage0(1)
+    next_part(0)
+    stage0(2)
+    stage0(0)
     stage1(1)
-    stage0(0)
-    next_a()
-    stage0(2)
+    next_part(1)
+    stage1(2)
+    stage0(3)
     stage1(0)
-    next_b()
-    stage1(2)
+    next_part(2)
+    stage2(2)
     prev()
-    stage0(3)
+    stage0(4)
+    stage1(3)
     turn_prev()
-    stage0(8)
-    stage2(2)
-    stage1(3)
-    stage1(8)
-    mate()
+    stage0(9)
+    stage1(4)
     stage2(3)
     stage3(2)
+    mate()
+    stage1(9)
     turn_mate()
-    stage2(8)
     stage0(6)
-    stage0(4)
-    stage2(0)
-    stage3(3)
+    stage2(4)
+    stage0(7)
     stage4(2)
     stage0(5)
-    stage0(7)
+    stage3(3)
     stage1(6)
-    stage1(4)
+    stage3(4)
+    stage1(7)
+    stage2(9)
+    stage4(3)
+    stage9(5)
+    stage4(4)
+    stage0(8)
+    stage2(7)
+    stage3(9)
+    stage5(3)
     stage1(5)
+    stage2(1)
+    stage5(4)
+    stage1(8)
+    stage5(2)
     stage2(6)
-    stage3(8)
-    stage2(4)
-    stage1(7)
-    stage4(3)
-    stage4(8)
-    stage5(2)
-    stage2(5)
-    stage3(4)
-    stage2(7)
-    stage5(3)
+    stage4(9)
+    stage3(5)
+    stage3(7)
+    stage6(1)
+    stage2(8)
+    stage5(9)
+    stage4(5)
     stage3(6)
-    stage5(8)
-    stage6(1)
-    stage3(5)
     stage6(4)
     give_back(NEXT, above)
-    stage3(7)
-    stage2(1)
-    stage4(4)
-    stage4(5)
+    stage3(8)
+    stage5(5)
+    stage4(7)
     stage4(6)
-    stage4(7)
-    stage8(4)
-    stage5(4)
-    stage3(1)
-    stage3(0)
-    stage5(5)
+    stage8(1)
+    stage2(0)
+    stage4(8)
+    stage7(5)
     stage5(6)
     stage5(7)
+    stage3(1)
+    stage8(4)
+    stage5(8)
     stage6(2)
     stage6(3)
     give_back(MATE, giver)
     stage8(3)
     give_back(PREV, below)
+    stage3(0)
     stage4(1)
-    stage8(1)
+    stage5(1)
     stage8(2)
-    stage5(1)
     stage4(0)
     stage5(0)
     stage6(0)
@@ -444,9 +489,10 @@
             pltpu.VMEM((JOBS, PIECE, NVIR), bf16),
             pltpu.VMEM((JOBS, PIECE, NVIR), bf16),
             pltpu.VMEM((JOBS, PIECE, NVIR), bf16),
+            pltpu.VMEM((max(1, len(CROSSED)), HALF, 256), bf16),
             pltpu.VMEM((3, ROWS, NVIR), bf16),
             pltpu.VMEM((3, ROWS, NVIR), bf16),
-            dma((len(CHUNKS), 13)), dma((len(CHUNKS), 13)), dma((13,)), dma((13,)),
+            dma((len(CHUNKS), 19)), dma((len(CHUNKS), 19)), dma((16,)), dma((16,)),
         ],
         compiler_params=pltpu.CompilerParams(
             collective_id=0, has_side_effects=True, vmem_limit_bytes=56 * 2**20

time: 96.5 us -> 93.6 us (0.970)
  Pallas kernels: 93.7 us -> 90.2 us
    pallas_call x1, Pallas kernels: 93.7 us -> 90.2 us  [on_device(): pl.pallas_call(kernel, out_shape=jax.ShapeDtypeStruct((ROWS, NVIR), bf16)...]
where the time goes in v6:
time: 93.6 us; the launch traced here: 92.7 us
  Pallas kernels  90.2 us (96%)
  local copies, waits for them, and re-layouts  1.91 us (2%)
    pallas_call x1, Pallas kernels, on_device(): pl.pallas_call(kernel, out_shape=jax.ShapeDtypeStruct((ROWS, NVIR), bf16)...  90.2 us
    unnamed x1, local copies, waits for them, and re-layouts  1.91 us

profile of v6, /device:TPU:1, one launch (start us, length us, event | category | flops | bytes accessed | tf_op | source)
XLA Modules:
  0.0 92.7 jit_solution(11834491783897900701)
XLA Ops:
  0.7 90.2 %shard_map.55 = bf16[320,896]{1,0:T(8,128)(2,1)} custom-call(s32[1]{0:T(128)S(6)} %copy.7.count_ref, s32[8]{0:T(128)} %pick_ref.1, f32[100]{0:T(128)} %occ_ref.1, f32[896]{0:T(1024)} %vir.1, bf16[320,896]{1,0:T(8,128)(2,1)} %bitcast.3), custom_call_target="tpu_custom_call" | custom-call | tf_op jit(solution)/shard_map/pallas_call | solution.py:467
  90.8 1.9 %copy.8 = bf16[320,1,896]{2,0,1:T(8,128)(2,1)} copy(bf16[320,1,896]{2,0,1:T(8,128)(2,1)} %bitcast.2) | data formatting | bytes 1146880

commit v7 on v6

--- a/solution.py
+++ b/solution.py
@@ -27,7 +27,7 @@
     count_ref, pick_ref, occ_ref, vir, b_ref, out,
     count, pick, occ, small,
     rows, flipped, acc, amp, virc, virr, partial, whole, half_whole,
-    z1_up, z1_down, z2_up, z2_down, mine, other, crossing, back_out, back_in,
+    z1_up, z1_down, z2_up, z2_down, mine, other, crossing, back_out, back_in, result,
     send, recv, b_send, b_recv,
 ):
     blk, grp = lax.axis_index("blk"), lax.axis_index("grp")
@@ -111,10 +111,10 @@
     pieces = range(len(PARTS))
     copies["own"] = spread(OWN, everything, 0, sibling)
     for i in pieces:
-        copies["next", i] = spread(NEXT, pl.ds(*PARTS[i]), 7 + i, below)
+        copies["next", i] = spread(NEXT, pl.ds(*PARTS[i]), 10 + i, below)
     copies["prev"] = spread(PREV, everything, 1, above)
     for i in pieces:
-        copies["mate", i] = to_partner(pl.ds(*PARTS[i]), 13 + i)
+        copies["mate", i] = to_partner(pl.ds(*PARTS[i]), 16 + i)
 
     @pl.when(lo == 1)
     def _():
@@ -186,7 +186,7 @@
 
     def next_part(i):
         copies["next", i].wait_recv()
-        copies["next on", i] = pass_on(NEXT, pl.ds(*PARTS[i]), 10 + i)
+        copies["next on", i] = pass_on(NEXT, pl.ds(*PARTS[i]), 13 + i)
         pl.when(lo == 0)(copies["mate", i].start)
 
     def prev():
@@ -363,99 +363,109 @@
                 rows[left[job], own_part, :], amp[job], preferred_element_type=jnp.float32
             )
 
+    halves = (pl.ds(0, ROWS // 2), pl.ds(ROWS // 2, ROWS // 2))
+
     def give_back(slot, device):
         index = slot - 1
-        back_out[index] = acc[slot].astype(jnp.bfloat16)
-        copies[slot] = start(
-            back_out.at[index], back_in.at[index], b_send.at[4 + index], b_recv.at[4 + index], device
-        )
+        for h, lines in enumerate(halves):
+            back_out[index, lines, :] = acc[slot, lines, :].astype(jnp.bfloat16)
+            copies[slot, h] = start(
+                back_out.at[index, lines], back_in.at[index, lines],
+                b_send.at[4 + 2 * index + h], b_recv.at[4 + 2 * index + h], device,
+            )
 
     own()
     stage0(1)
+    stage0(0)
     next_part(0)
+    stage1(1)
     stage0(2)
-    stage0(0)
-    stage1(1)
+    stage1(0)
     next_part(1)
+    stage0(3)
     stage1(2)
-    stage0(3)
-    stage1(0)
     next_part(2)
+    stage1(3)
+    prev()
     stage2(2)
-    prev()
     stage0(4)
-    stage1(3)
     turn_prev()
+    stage2(3)
     stage0(9)
     stage1(4)
-    stage2(3)
     stage3(2)
+    stage3(3)
+    stage2(4)
+    stage1(9)
     mate()
-    stage1(9)
+    stage4(2)
+    stage4(3)
     turn_mate()
     stage0(6)
-    stage2(4)
     stage0(7)
-    stage4(2)
     stage0(5)
-    stage3(3)
+    stage3(4)
+    stage0(8)
+    stage1(7)
     stage1(6)
-    stage3(4)
-    stage1(7)
     stage2(9)
-    stage4(3)
+    stage1(8)
     stage9(5)
+    stage2(7)
+    stage5(2)
+    stage2(0)
+    stage3(9)
+    stage2(6)
+    stage1(5)
     stage4(4)
-    stage0(8)
-    stage2(7)
-    stage3(9)
+    stage2(8)
+    stage4(9)
+    stage2(1)
+    stage3(5)
     stage5(3)
-    stage1(5)
-    stage2(1)
     stage5(4)
-    stage1(8)
-    stage5(2)
-    stage2(6)
-    stage4(9)
-    stage3(5)
     stage3(7)
+    stage5(9)
+    stage3(6)
     stage6(1)
-    stage2(8)
-    stage5(9)
     stage4(5)
-    stage3(6)
     stage6(4)
     give_back(NEXT, above)
+    stage8(4)
     stage3(8)
     stage5(5)
+    stage4(6)
     stage4(7)
-    stage4(6)
-    stage8(1)
-    stage2(0)
     stage4(8)
+    stage5(6)
     stage7(5)
-    stage5(6)
     stage5(7)
-    stage3(1)
-    stage8(4)
     stage5(8)
+    stage3(0)
     stage6(2)
     stage6(3)
     give_back(MATE, giver)
     stage8(3)
     give_back(PREV, below)
-    stage3(0)
+    stage8(1)
+    stage4(0)
+    stage3(1)
+    stage5(0)
     stage4(1)
     stage5(1)
     stage8(2)
-    stage4(0)
-    stage5(0)
     stage6(0)
-    for slot in (NEXT, PREV, MATE):
-        copies[slot].wait_recv()
-    total = acc[OWN] + back_in[0].astype(jnp.float32)
-    total = total + back_in[1].astype(jnp.float32) + back_in[2].astype(jnp.float32)
-    out[...] = total.astype(jnp.bfloat16)
+    stores = []
+    for h, lines in enumerate(halves):
+        for slot in (NEXT, PREV, MATE):
+            copies[slot, h].wait_recv()
+        total = acc[OWN, lines, :] + back_in[0, lines, :].astype(jnp.float32)
+        total = total + back_in[1, lines, :].astype(jnp.float32) + back_in[2, lines, :].astype(jnp.float32)
+        result[lines, :] = total.astype(jnp.bfloat16)
+        stores.append(pltpu.make_async_copy(result.at[lines], out.at[lines], small.at[4 + h]))
+        stores[h].start()
+    for store in stores:
+        store.wait()
     for copy in started:
         copy.wait_send()
 
@@ -468,12 +478,12 @@
         kernel,
         out_shape=jax.ShapeDtypeStruct((ROWS, NVIR), bf16),
         in_specs=[hbm, hbm, hbm, vmem, hbm],
-        out_specs=vmem,
+        out_specs=hbm,
         scratch_shapes=[
             pltpu.SMEM((1,), jnp.int32),
             pltpu.SMEM((8,), jnp.int32),
             pltpu.SMEM((100,), f32),
-            dma((4,)),
+            dma((6,)),
             pltpu.VMEM((4, 2 * ROWS, NVIR), bf16),
             pltpu.VMEM((3, NVIR, 2 * ROWS), bf16),
             pltpu.VMEM((4, ROWS, NVIR), f32),
@@ -492,7 +502,8 @@
             pltpu.VMEM((max(1, len(CROSSED)), HALF, 256), bf16),
             pltpu.VMEM((3, ROWS, NVIR), bf16),
             pltpu.VMEM((3, ROWS, NVIR), bf16),
-            dma((len(CHUNKS), 19)), dma((len(CHUNKS), 19)), dma((16,)), dma((16,)),
+            pltpu.VMEM((ROWS, NVIR), bf16),
+            dma((len(CHUNKS), 19)), dma((len(CHUNKS), 19)), dma((19,)), dma((19,)),
         ],
         compiler_params=pltpu.CompilerParams(
             collective_id=0, has_side_effects=True, vmem_limit_bytes=56 * 2**20

time: 93.6 us -> 95.5 us (1.020)
  Pallas kernels: 90.2 us -> 92.7 us
    pallas_call x1, Pallas kernels: 90.2 us -> 92.7 us  [on_device(): pl.pallas_call(kernel, out_shape=jax.ShapeDtypeStruct((ROWS, NVIR), bf16)...]
where the time goes in v7:
time: 95.5 us; the launch traced here: 95.3 us
  Pallas kernels  92.7 us (97%)
  local copies, waits for them, and re-layouts  1.91 us (2%)
    pallas_call x1, Pallas kernels, on_device(): pl.pallas_call(kernel, out_shape=jax.ShapeDtypeStruct((ROWS, NVIR), bf16)...  92.7 us
    unnamed x1, local copies, waits for them, and re-layouts  1.91 us

profile of v7, /device:TPU:1, one launch (start us, length us, event | category | flops | bytes accessed | tf_op | source)
XLA Modules:
  0.0 95.3 jit_solution(14047579424641934830)
XLA Ops:
  0.7 92.7 %shard_map.55 = bf16[320,896]{1,0:T(8,128)(2,1)} custom-call(s32[1]{0:T(128)S(6)} %copy.7.count_ref, s32[8]{0:T(128)} %pick_ref.1, f32[100]{0:T(128)} %occ_ref.1, f32[896]{0:T(1024)} %vir.1, bf16[320,896]{1,0:T(8,128)(2,1)} %bitcast.3), custom_call_target="tpu_custom_call" | custom-call | tf_op jit(solution)/shard_map/pallas_call | solution.py:477
  93.4 1.9 %copy.8 = bf16[320,1,896]{2,0,1:T(8,128)(2,1)} copy(bf16[320,1,896]{2,0,1:T(8,128)(2,1)} %bitcast.2) | data formatting | bytes 1146880

commit v8 on v6

--- a/solution.py
+++ b/solution.py
@@ -24,10 +24,10 @@
 
 
 def kernel(
-    count_ref, pick_ref, occ_ref, vir, b_ref, out,
-    count, pick, occ, small,
+    count_ref, pick_ref, occ_ref, vir_ref, b_ref, out,
+    count, pick, occ, vir, small,
     rows, flipped, acc, amp, virc, virr, partial, whole, half_whole,
-    z1_up, z1_down, z2_up, z2_down, mine, other, crossing, back_out, back_in,
+    z1_up, z1_down, z2_up, z2_down, mine, other, crossing, back_out, back_in, result,
     send, recv, b_send, b_recv,
 ):
     blk, grp = lax.axis_index("blk"), lax.axis_index("grp")
@@ -60,27 +60,28 @@
         copy.start()
         return copy
 
-    fetches = [
-        pltpu.make_async_copy(src, dst, small.at[index])
-        for index, (src, dst) in enumerate(
-            ((b_ref, rows.at[OWN, own_part]), (count_ref, count), (pick_ref, pick), (occ_ref, occ))
-        )
-    ]
-    for fetch in fetches:
-        fetch.start()
-    half_whole[...] = jnp.zeros_like(half_whole)
-
     barrier = pltpu.get_barrier_semaphore()
     everyone = (sibling, above, below, partner, diagonal, far, up, down)
     for device in everyone:
         pl.semaphore_signal(barrier, inc=1, device_id=device, device_id_type=MESH)
 
+    fetches = [
+        pltpu.make_async_copy(src, dst, small.at[index])
+        for index, (src, dst) in enumerate(
+            (
+                (b_ref, rows.at[OWN, own_part]), (count_ref, count), (vir_ref, vir),
+                (pick_ref, pick), (occ_ref, occ),
+            )
+        )
+    ]
+    for fetch in fetches:
+        fetch.start()
+
+    half_whole[...] = jnp.zeros_like(half_whole)
     acc[...] = jnp.zeros_like(acc)
-    virc[...] = jnp.transpose(jnp.broadcast_to(vir[...].reshape(1, NVIR), (128, NVIR)))
-    virr[...] = jnp.broadcast_to(vir[...].reshape(1, NVIR), (8, NVIR))
-
-    for fetch in fetches:
-        fetch.wait()
+
+    fetches[0].wait()
+    fetches[1].wait()
     line = lax.broadcasted_iota(jnp.int32, (ROWS, NVIR), 0)
     live = jnp.where(line < count[0], rows[OWN, own_part, :].astype(jnp.float32), 0.0)
     rows[OWN, own_part, :] = live.astype(jnp.bfloat16)
@@ -111,15 +112,20 @@
     pieces = range(len(PARTS))
     copies["own"] = spread(OWN, everything, 0, sibling)
     for i in pieces:
-        copies["next", i] = spread(NEXT, pl.ds(*PARTS[i]), 7 + i, below)
+        copies["next", i] = spread(NEXT, pl.ds(*PARTS[i]), 10 + i, below)
     copies["prev"] = spread(PREV, everything, 1, above)
     for i in pieces:
-        copies["mate", i] = to_partner(pl.ds(*PARTS[i]), 13 + i)
+        copies["mate", i] = to_partner(pl.ds(*PARTS[i]), 16 + i)
 
     @pl.when(lo == 1)
     def _():
         for i in pieces:
             copies["mate", i].start()
+
+    for fetch in fetches[2:]:
+        fetch.wait()
+    virc[...] = jnp.transpose(jnp.broadcast_to(vir[...].reshape(1, NVIR), (128, NVIR)))
+    virr[...] = jnp.broadcast_to(vir[...].reshape(1, NVIR), (8, NVIR))
 
     def energy(position):
         return occ[pick[position]]
@@ -186,7 +192,7 @@
 
     def next_part(i):
         copies["next", i].wait_recv()
-        copies["next on", i] = pass_on(NEXT, pl.ds(*PARTS[i]), 10 + i)
+        copies["next on", i] = pass_on(NEXT, pl.ds(*PARTS[i]), 13 + i)
         pl.when(lo == 0)(copies["mate", i].start)
 
     def prev():
@@ -363,12 +369,16 @@
                 rows[left[job], own_part, :], amp[job], preferred_element_type=jnp.float32
             )
 
+    halves = (pl.ds(0, ROWS // 2), pl.ds(ROWS // 2, ROWS // 2))
+
     def give_back(slot, device):
         index = slot - 1
-        back_out[index] = acc[slot].astype(jnp.bfloat16)
-        copies[slot] = start(
-            back_out.at[index], back_in.at[index], b_send.at[4 + index], b_recv.at[4 + index], device
-        )
+        for h, lines in enumerate(halves):
+            back_out[index, lines, :] = acc[slot, lines, :].astype(jnp.bfloat16)
+            copies[slot, h] = start(
+                back_out.at[index, lines], back_in.at[index, lines],
+                b_send.at[4 + 2 * index + h], b_recv.at[4 + 2 * index + h], device,
+            )
 
     own()
     stage0(1)
@@ -451,29 +461,36 @@
     stage4(0)
     stage5(0)
     stage6(0)
-    for slot in (NEXT, PREV, MATE):
-        copies[slot].wait_recv()
-    total = acc[OWN] + back_in[0].astype(jnp.float32)
-    total = total + back_in[1].astype(jnp.float32) + back_in[2].astype(jnp.float32)
-    out[...] = total.astype(jnp.bfloat16)
+    stores = []
+    for h, lines in enumerate(halves):
+        for slot in (NEXT, PREV, MATE):
+            copies[slot, h].wait_recv()
+        total = acc[OWN, lines, :] + back_in[0, lines, :].astype(jnp.float32)
+        total = total + back_in[1, lines, :].astype(jnp.float32) + back_in[2, lines, :].astype(jnp.float32)
+        result[lines, :] = total.astype(jnp.bfloat16)
+        stores.append(pltpu.make_async_copy(result.at[lines], out.at[lines], small.at[5 + h]))
+        stores[h].start()
+    for store in stores:
+        store.wait()
     for copy in started:
         copy.wait_send()
 
 
 def on_device(b_rows, aux_count, occ_pick, eps_occ, eps_vir):
     bf16, f32 = jnp.bfloat16, jnp.float32
-    hbm, vmem = pl.BlockSpec(memory_space=pl.ANY), pl.BlockSpec(memory_space=pltpu.VMEM)
+    hbm = pl.BlockSpec(memory_space=pl.ANY)
     dma = pltpu.SemaphoreType.DMA
     gamma = pl.pallas_call(
         kernel,
         out_shape=jax.ShapeDtypeStruct((ROWS, NVIR), bf16),
-        in_specs=[hbm, hbm, hbm, vmem, hbm],
-        out_specs=vmem,
+        in_specs=[hbm] * 5,
+        out_specs=hbm,
         scratch_shapes=[
             pltpu.SMEM((1,), jnp.int32),
             pltpu.SMEM((8,), jnp.int32),
             pltpu.SMEM((100,), f32),
-            dma((4,)),
+            pltpu.VMEM((NVIR,), f32),
+            dma((7,)),
             pltpu.VMEM((4, 2 * ROWS, NVIR), bf16),
             pltpu.VMEM((3, NVIR, 2 * ROWS), bf16),
             pltpu.VMEM((4, ROWS, NVIR), f32),
@@ -492,7 +509,8 @@
             pltpu.VMEM((max(1, len(CROSSED)), HALF, 256), bf16),
             pltpu.VMEM((3, ROWS, NVIR), bf16),
             pltpu.VMEM((3, ROWS, NVIR), bf16),
-            dma((len(CHUNKS), 19)), dma((len(CHUNKS), 19)), dma((16,)), dma((16,)),
+            pltpu.VMEM((ROWS, NVIR), bf16),
+            dma((len(CHUNKS), 19)), dma((len(CHUNKS), 19)), dma((19,)), dma((19,)),
         ],
         compiler_params=pltpu.CompilerParams(
             collective_id=0, has_side_effects=True, vmem_limit_bytes=56 * 2**20

time: 93.6 us -> 92.8 us (level)
  no operation moved by 1% of the time
where the time goes in v8:
time: 92.8 us; the launch traced here: 92 us
  Pallas kernels  89.4 us (96%)
  local copies, waits for them, and re-layouts  1.91 us (2%)
    pallas_call x1, Pallas kernels, on_device(): pl.pallas_call(kernel, out_shape=jax.ShapeDtypeStruct((ROWS, NVIR), bf16)...  89.4 us
    unnamed x1, local copies, waits for them, and re-layouts  1.91 us

profile of v8, /device:TPU:1, one launch (start us, length us, event | category | flops | bytes accessed | tf_op | source)
XLA Modules:
  0.0 92.0 jit_solution(11838352798635771411)
XLA Ops:
  0.7 89.4 %shard_map.55 = bf16[320,896]{1,0:T(8,128)(2,1)} custom-call(s32[1]{0:T(128)S(6)} %copy.7.count_ref, s32[8]{0:T(128)} %pick_ref.1, f32[100]{0:T(128)} %occ_ref.1, f32[896]{0:T(1024)} %vir_ref.1, bf16[320,896]{1,0:T(8,128)(2,1)} %bitcast.3), custom_call_target="tpu_custom_call" | custom-call | tf_op jit(solution)/shard_map/pallas_call | solution.py:483
  90.0 1.9 %copy.8 = bf16[320,1,896]{2,0,1:T(8,128)(2,1)} copy(bf16[320,1,896]{2,0,1:T(8,128)(2,1)} %bitcast.2) | data formatting | bytes 1146880

commit v9 on v8

--- a/solution.py
+++ b/solution.py
@@ -352,33 +352,43 @@
             return carry
 
         lax.fori_loop(0, NVIR // 128, body, 0, unroll=True)
-        apply(job, first_side[job])
+        if job == 3:
+            for h, lines in enumerate(halves):
+                apply(job, first_side[job], lines)
+                give_half(MATE, h, giver)
+        else:
+            apply(job, first_side[job])
 
     def stage8(job):
         apply(job, 1 - first_side[job])
 
     first_side = (0, 1, 0, 0, 1)
 
-    def apply(job, side):
+    def apply(job, side, lines=pl.ds(0, ROWS)):
+        mine_here = pl.ds(pl.multiple_of(core * ROWS + lines.start, 16), lines.size)
         if side == 0:
-            acc[left[job]] = acc[left[job]] + lax.dot_general(
-                rows[right[job], own_part, :], amp[job], (((1,), (1,)), ((), ())), preferred_element_type=jnp.float32
+            acc[left[job], lines, :] = acc[left[job], lines, :] + lax.dot_general(
+                rows[right[job], mine_here, :], amp[job], (((1,), (1,)), ((), ())),
+                preferred_element_type=jnp.float32,
             )
         else:
-            acc[right[job]] = acc[right[job]] + jnp.dot(
-                rows[left[job], own_part, :], amp[job], preferred_element_type=jnp.float32
+            acc[right[job], lines, :] = acc[right[job], lines, :] + jnp.dot(
+                rows[left[job], mine_here, :], amp[job], preferred_element_type=jnp.float32
             )
 
     halves = (pl.ds(0, ROWS // 2), pl.ds(ROWS // 2, ROWS // 2))
 
+    def give_half(slot, h, device):
+        index, lines = slot - 1, halves[h]
+        back_out[index, lines, :] = acc[slot, lines, :].astype(jnp.bfloat16)
+        copies[slot, h] = start(
+            back_out.at[index, lines], back_in.at[index, lines],
+            b_send.at[4 + 2 * index + h], b_recv.at[4 + 2 * index + h], device,
+        )
+
     def give_back(slot, device):
-        index = slot - 1
-        for h, lines in enumerate(halves):
-            back_out[index, lines, :] = acc[slot, lines, :].astype(jnp.bfloat16)
-            copies[slot, h] = start(
-                back_out.at[index, lines], back_in.at[index, lines],
-                b_send.at[4 + 2 * index + h], b_recv.at[4 + 2 * index + h], device,
-            )
+        for h in range(len(halves)):
+            give_half(slot, h, device)
 
     own()
     stage0(1)
@@ -447,11 +457,10 @@
     stage5(6)
     stage5(7)
     stage3(1)
+    stage5(8)
     stage8(4)
-    stage5(8)
     stage6(2)
     stage6(3)
-    give_back(MATE, giver)
     stage8(3)
     give_back(PREV, below)
     stage3(0)
@@ -461,6 +470,7 @@
     stage4(0)
     stage5(0)
     stage6(0)
+
     stores = []
     for h, lines in enumerate(halves):
         for slot in (NEXT, PREV, MATE):

time: 92.8 us -> 92.8 us (level)
  no operation moved by 1% of the time
where the time goes in v9:
time: 92.8 us; the launch traced here: 91.5 us
  Pallas kernels  88.9 us (96%)
  local copies, waits for them, and re-layouts  1.91 us (2%)
    pallas_call x1, Pallas kernels, on_device(): pl.pallas_call(kernel, out_shape=jax.ShapeDtypeStruct((ROWS, NVIR), bf16)...  88.9 us
    unnamed x1, local copies, waits for them, and re-layouts  1.91 us

profile of v9, /device:TPU:1, one launch (start us, length us, event | category | flops | bytes accessed | tf_op | source)
XLA Modules:
  0.0 91.5 jit_solution(6909807200343181616)
XLA Ops:
  0.7 88.9 %shard_map.55 = bf16[320,896]{1,0:T(8,128)(2,1)} custom-call(s32[1]{0:T(128)S(6)} %copy.7.count_ref, s32[8]{0:T(128)} %pick_ref.1, f32[100]{0:T(128)} %occ_ref.1, f32[896]{0:T(1024)} %vir_ref.1, bf16[320,896]{1,0:T(8,128)(2,1)} %bitcast.3), custom_call_target="tpu_custom_call" | custom-call | tf_op jit(solution)/shard_map/pallas_call | solution.py:493
  89.6 1.9 %copy.8 = bf16[320,1,896]{2,0,1:T(8,128)(2,1)} copy(bf16[320,1,896]{2,0,1:T(8,128)(2,1)} %bitcast.2) | data formatting | bytes 1146880

commit v10 on v9

--- a/solution.py
+++ b/solution.py
@@ -360,7 +360,12 @@
             apply(job, first_side[job])
 
     def stage8(job):
-        apply(job, 1 - first_side[job])
+        if job == 3:
+            for h, lines in enumerate(halves):
+                apply(job, 1 - first_side[job], lines)
+                give_half(PREV, h, below)
+        else:
+            apply(job, 1 - first_side[job])
 
     first_side = (0, 1, 0, 0, 1)
 
@@ -462,7 +467,6 @@
     stage6(2)
     stage6(3)
     stage8(3)
-    give_back(PREV, below)
     stage3(0)
     stage4(1)
     stage5(1)

time: 92.8 us -> 92.8 us (level)
  no operation moved by 1% of the time
where the time goes in v10:
time: 92.8 us; the launch traced here: 91.7 us
  Pallas kernels  89.1 us (96%)
  local copies, waits for them, and re-layouts  1.91 us (2%)
    pallas_call x1, Pallas kernels, on_device(): pl.pallas_call(kernel, out_shape=jax.ShapeDtypeStruct((ROWS, NVIR), bf16)...  89.1 us
    unnamed x1, local copies, waits for them, and re-layouts  1.91 us

profile of v10, /device:TPU:1, one launch (start us, length us, event | category | flops | bytes accessed | tf_op | source)
XLA Modules:
  0.0 91.7 jit_solution(507022598951258674)
XLA Ops:
  0.7 89.1 %shard_map.55 = bf16[320,896]{1,0:T(8,128)(2,1)} custom-call(s32[1]{0:T(128)S(6)} %copy.7.count_ref, s32[8]{0:T(128)} %pick_ref.1, f32[100]{0:T(128)} %occ_ref.1, f32[896]{0:T(1024)} %vir_ref.1, bf16[320,896]{1,0:T(8,128)(2,1)} %bitcast.3), custom_call_target="tpu_custom_call" | custom-call | tf_op jit(solution)/shard_map/pallas_call | solution.py:497
  89.7 1.9 %copy.8 = bf16[320,1,896]{2,0,1:T(8,128)(2,1)} copy(bf16[320,1,896]{2,0,1:T(8,128)(2,1)} %bitcast.2) | data formatting | bytes 1146880
